TPU v7x, 32 devices: a whole 2x2x4 slice. The times are simulated.
32 devices in a mesh: section: 2 (over x), dp: 8 (over z, y), tensor: 2 (over core).
Axes of the slice: x: 2, y: 2, z: 4, core: 2. Of those that a mesh axis runs over, the one named last changes fastest.
Arguments:
- frames: bfloat16 [4, 1024, 1024], P(None, 'dp'), may hold values from -6 to 6
- codes: int32 [4, 1024, 3], P(None, 'dp'), may hold values from 0 to 1023
- lengths: int32 [4, 16], replicated, may hold values from 0 to 1024, as said below
- gains: float32 [2, 2, 1024], P('section'), may hold values from 0.5 to 1.5
- w_qkv: bfloat16 [2, 1024, 3, 1024], P('section', None, None, 'tensor'), may hold values from -0.1875 to 0.1875
- w_out: bfloat16 [2, 1024, 1024], P('section', 'tensor'), may hold values from -0.5 to 0.5
- w_up: bfloat16 [2, 1024, 4096], P('section', None, 'tensor'), may hold values from -0.1875 to 0.1875
- w_down: bfloat16 [2, 4096, 1024], P('section', 'tensor'), may hold values from -0.09375 to 0.09375
- table: bfloat16 [3, 1024, 1024], replicated, may hold values from -6 to 6
- cotangent: bfloat16 [4, 1024, 3, 1024], P(None, 'dp'), may hold values from -6 to 6
Outputs:
- global_out: bfloat16 [4, 1024, 1024], P(None, 'dp')
- local_out: bfloat16 [4, 1024, 3, 1024], P(None, 'dp')
- input_grads: float32 [2, 4, 1024, 1024], P('section', None, 'dp')
- grad_qkv: float32 [2, 1024, 3, 1024], P('section', 'dp', None, 'tensor')
- grad_out: float32 [2, 1024, 1024], P('section', 'tensor', 'dp')
- grad_up: float32 [2, 1024, 4096], P('section', 'dp', 'tensor')
- grad_down: float32 [2, 4096, 1024], P('section', 'tensor', 'dp')
- grad_gains: float32 [2, 2, 1024], P('section', None, 'dp')
- grad_table: float32 [3, 1024, 1024], P(None, ('section', 'dp'))
Inputs may be any that keep to these rules, and one draw needn't show every extreme that they name: In every draw one micro-batch, drawn from the seed, holds a single sequence of 1024 frames; in the others the lengths add up to less than 1024 and the frames after the last sequence are padding. A slot of length 0 is unused.
All inputs are finite; a program needn't handle non-finite values.
Results may differ from a plain program's by a relative error of at most 0.015.
Values may be sent and summed in bfloat16 or wider, within the bound.
No kernel may reach another device: no remote copies, remote signals or barrier semaphores. Data moves between devices by JAX's collectives and lax.ppermute only.
A program may use at most 256 MiB of HBM per device.

v0:
```python
import functools

import jax
import jax.numpy as jnp
from jax import lax
from jax.experimental import pallas as pl
from jax.experimental.pallas import tpu as pltpu
from jax.sharding import PartitionSpec as P

HEAD = 64
CODEBOOKS = 3


eps = 1e-05
far = -1e30


def from_behind(block, axis, distance):
    devices = range(lax.axis_size(axis))
    route = [(i - distance, i) for i in devices if i - distance in devices]
    return lax.ppermute(block, axis, route)


def rms_scale(values):
    return lax.rsqrt(jnp.mean(values * values, axis=-1, keepdims=True) + eps)


def rms_back(values, gain_row, grad_normed):
    factor = rms_scale(values)
    normal = values * factor
    grad_unit = grad_normed * gain_row
    grad_values = factor * (
        grad_unit - normal * jnp.mean(grad_unit * normal, axis=-1, keepdims=True)
    )
    return (grad_values, jnp.sum(grad_normed * normal, axis=0))


def head_total(partial_sum):
    return lax.psum(partial_sum, "tensor")


def matmul(left, right):
    return jnp.dot(left, right, preferred_element_type=jnp.float32)


def across_rows(left, right):
    return lax.dot_general(
        left, right, (((0,), (0,)), ((), ())), preferred_element_type=jnp.float32
    )


def against_rows(left, right):
    return lax.dot_general(
        left, right, (((1,), (1,)), ((), ())), preferred_element_type=jnp.float32
    )


def smooth_gate(values):
    return jax.nn.gelu(values, approximate=True)


def doc_index(positions, doc_ends):
    return jnp.sum((positions[:, None] >= doc_ends[None, :]).astype(jnp.int32), axis=1)


def allowed_mask(query_pos, key_pos, doc_ends):
    same_doc = doc_index(query_pos, doc_ends)[:, None] == doc_index(key_pos, doc_ends)[None, :]
    earlier = key_pos[None, :] <= query_pos[:, None]
    live = (key_pos < doc_ends[-1])[None, :]
    return same_doc & earlier & live | (key_pos[None, :] == query_pos[:, None])


def masked_softmax(scores, mask, factor):
    logits = jnp.where(mask, scores * factor, far)
    top = jnp.max(logits, axis=-1, keepdims=True)
    weights = jnp.exp(logits - top)
    mass = jnp.sum(weights, axis=-1, keepdims=True)
    return (weights / mass, (top + jnp.log(mass))[..., 0])


def frame_forward(packed, query_pos, doc_ends, head_count):
    row_count = packed.shape[0]
    width = packed.shape[1] // 3
    factor = HEAD ** (-0.5)
    parts = packed.reshape(row_count, 3, width)
    all_keys, all_values = (
        lax.all_gather(parts[:, 1], "dp", axis=0, tiled=True),
        lax.all_gather(parts[:, 2], "dp", axis=0, tiled=True),
    )
    key_count = all_keys.shape[0]
    key_pos = jnp.arange(key_count, dtype=jnp.int32)
    mask = allowed_mask(query_pos, key_pos, doc_ends)
    queries = parts[:, 0].reshape(row_count, head_count, -1)
    scores = jnp.einsum(
        "qhe,khe->hqk",
        queries,
        all_keys.reshape(key_count, head_count, -1),
        preferred_element_type=jnp.float32,
    )
    probs, log_mass = masked_softmax(scores, mask[None], factor)
    attended = jnp.einsum(
        "hqk,khe->qhe",
        probs.astype(jnp.bfloat16),
        all_values.reshape(key_count, head_count, -1),
        preferred_element_type=jnp.float32,
    )
    return (attended.reshape(row_count, width), log_mass)


def frame_backward(packed, grad_att, log_mass, query_pos, doc_ends, head_count):
    row_count = packed.shape[0]
    width = packed.shape[1] // 3
    factor = HEAD ** (-0.5)
    parts = packed.reshape(row_count, 3, width)
    all_keys, all_values = (
        lax.all_gather(parts[:, 1], "dp", axis=0, tiled=True),
        lax.all_gather(parts[:, 2], "dp", axis=0, tiled=True),
    )
    key_count = all_keys.shape[0]
    key_pos = jnp.arange(key_count, dtype=jnp.int32)
    queries = parts[:, 0].reshape(row_count, head_count, -1)
    grad_heads = grad_att.reshape(row_count, head_count, -1)
    keys_heads = all_keys.reshape(key_count, head_count, -1)
    scores = jnp.einsum("qhe,khe->hqk", queries, keys_heads, preferred_element_type=jnp.float32)
    mask = allowed_mask(query_pos, key_pos, doc_ends)
    probs = jnp.exp(jnp.where(mask[None], scores * factor, far) - log_mass[:, :, None])
    grad_probs = jnp.einsum(
        "qhe,khe->hqk",
        grad_heads,
        all_values.reshape(key_count, head_count, -1),
        preferred_element_type=jnp.float32,
    )
    spread = jnp.sum(probs * grad_probs, axis=-1)
    grad_scores = (probs * (grad_probs - spread[:, :, None]) * factor).astype(jnp.bfloat16)
    grad_queries = jnp.einsum(
        "hqk,khe->qhe", grad_scores, keys_heads, preferred_element_type=jnp.float32
    ).reshape(row_count, width)
    keys_term = jnp.einsum(
        "hqk,qhe->khe", grad_scores, queries, preferred_element_type=jnp.float32
    ).reshape(key_count, width)
    values_term = jnp.einsum(
        "hqk,qhe->khe", probs.astype(jnp.bfloat16), grad_heads, preferred_element_type=jnp.float32
    ).reshape(key_count, width)
    grad_keys, grad_values = (
        lax.psum_scatter(keys_term, "dp", scatter_dimension=0, tiled=True),
        lax.psum_scatter(values_term, "dp", scatter_dimension=0, tiled=True),
    )
    return jnp.stack([grad_queries, grad_keys, grad_values], axis=1).reshape(row_count, 3 * width)


def codebook_forward(packed, head_count):
    row_count = packed.shape[0]
    width = packed.shape[1] // 3
    factor = HEAD ** (-0.5)
    parts = packed.reshape(row_count // CODEBOOKS, CODEBOOKS, 3, head_count, -1)
    scores = jnp.einsum(
        "nche,ndhe->nhcd", parts[:, :, 0], parts[:, :, 1], preferred_element_type=jnp.float32
    )
    order = jnp.arange(CODEBOOKS, dtype=jnp.int32)
    mask = order[None, :] <= order[:, None]
    probs, log_mass = masked_softmax(scores, mask, factor)
    attended = jnp.einsum(
        "nhcd,ndhe->nche",
        probs.astype(jnp.bfloat16),
        parts[:, :, 2],
        preferred_element_type=jnp.float32,
    )
    return (attended.reshape(row_count, width), probs)


def codebook_backward(packed, grad_att, probs, head_count):
    row_count = packed.shape[0]
    width = packed.shape[1] // 3
    factor = HEAD ** (-0.5)
    parts = packed.reshape(row_count // CODEBOOKS, CODEBOOKS, 3, head_count, -1)
    grad_heads = grad_att.reshape(row_count // CODEBOOKS, CODEBOOKS, head_count, -1)
    grad_probs = jnp.einsum(
        "nche,ndhe->nhcd", grad_heads, parts[:, :, 2], preferred_element_type=jnp.float32
    )
    spread = jnp.sum(probs * grad_probs, axis=-1, keepdims=True)
    grad_scores = (probs * (grad_probs - spread) * factor).astype(jnp.bfloat16)
    grad_queries = jnp.einsum(
        "nhcd,ndhe->nche", grad_scores, parts[:, :, 1], preferred_element_type=jnp.float32
    )
    grad_keys = jnp.einsum(
        "nhcd,nche->ndhe", grad_scores, parts[:, :, 0], preferred_element_type=jnp.float32
    )
    grad_values = jnp.einsum(
        "nhcd,nche->ndhe",
        probs.astype(jnp.bfloat16),
        grad_heads,
        preferred_element_type=jnp.float32,
    )
    return jnp.stack([grad_queries, grad_keys, grad_values], axis=2).reshape(row_count, 3 * width)


def layer_forward(inputs, gain_pair, layer_weights, attend):
    w_proj, w_mix, w_rise, w_fall = layer_weights
    normed = (inputs * rms_scale(inputs) * gain_pair[0]).astype(jnp.bfloat16)
    packed = matmul(normed, w_proj.reshape(w_proj.shape[0], -1)).astype(jnp.bfloat16)
    attended, saved = attend(packed)
    attended_low = attended.astype(jnp.bfloat16)
    resid = inputs + head_total(matmul(attended_low, w_mix))
    normed_mid = (resid * rms_scale(resid) * gain_pair[1]).astype(jnp.bfloat16)
    rise = matmul(normed_mid, w_rise)
    active = smooth_gate(rise).astype(jnp.bfloat16)
    result = resid + head_total(matmul(active, w_fall))
    return (result, (normed, packed, attended_low, saved, resid, normed_mid, rise, active))


def layer_backward(inputs, gain_pair, layer_weights, kept, grad_result, attend_back):
    w_proj, w_mix, w_rise, w_fall = layer_weights
    normed, packed, attended_low, saved, resid, normed_mid, rise, active = kept
    grad_fall_low = grad_result.astype(jnp.bfloat16)
    grad_fall_w = across_rows(active, grad_fall_low)
    grad_active = against_rows(grad_fall_low, w_fall)
    grad_rise = jax.vjp(smooth_gate, rise)[1](grad_active)[0].astype(jnp.bfloat16)
    grad_rise_w = across_rows(normed_mid, grad_rise)
    grad_mid = head_total(against_rows(grad_rise, w_rise))
    back_mid, gain_mid = rms_back(resid, gain_pair[1], grad_mid)
    grad_resid = grad_result + back_mid
    resid_low = grad_resid.astype(jnp.bfloat16)
    grad_mix_w = across_rows(attended_low, resid_low)
    grad_att = against_rows(resid_low, w_mix).astype(jnp.bfloat16)
    grad_packed = attend_back(packed, grad_att, saved).astype(jnp.bfloat16)
    flat_proj = w_proj.reshape(w_proj.shape[0], -1)
    grad_proj_w = across_rows(normed, grad_packed).reshape(w_proj.shape)
    grad_normed = head_total(against_rows(grad_packed, flat_proj))
    back_in, gain_in = rms_back(inputs, gain_pair[0], grad_normed)
    return (
        grad_resid + back_in,
        (grad_proj_w, grad_mix_w, grad_rise_w, grad_fall_w, jnp.stack([gain_in, gain_mid])),
    )


def plain_body(frames, codes, lengths, gains, w_qkv, w_out, w_up, w_down, table, cotangent):
    on_first = lax.axis_index("section") == 0
    head_count = w_qkv.shape[3] // HEAD
    layer_weights = (w_qkv[0], w_out[0], w_up[0], w_down[0])
    gains_here = gains[0]
    frame_count = frames.shape[1]
    query_pos = lax.axis_index("dp") * frame_count + jnp.arange(frame_count, dtype=jnp.int32)
    zero_grads = (
        jnp.zeros(w_qkv.shape[1:], jnp.float32),
        jnp.zeros(w_out.shape[1:], jnp.float32),
        jnp.zeros(w_up.shape[1:], jnp.float32),
        jnp.zeros(w_down.shape[1:], jnp.float32),
        jnp.zeros(gains.shape[1:], jnp.float32),
    )

    def global_forward_rows(frame_rows, slot_lengths):
        doc_ends = jnp.cumsum(slot_lengths)
        return (
            doc_ends,
            layer_forward(
                frame_rows.astype(jnp.float32),
                gains_here,
                layer_weights,
                lambda packed: frame_forward(packed, query_pos, doc_ends, head_count),
            ),
        )

    def global_step(carry, inputs):
        doc_ends, (result, kept) = global_forward_rows(inputs[0], inputs[1])
        return (carry, result.astype(jnp.bfloat16))

    global_low = lax.scan(global_step, jnp.zeros((), jnp.int32), (frames, lengths))[1]
    arrived = from_behind(global_low, "section", 1)
    books = jnp.arange(CODEBOOKS, dtype=jnp.int32)
    looked_up = table[books[None, None, :], codes]
    local_in = arrived.astype(jnp.float32)[:, :, None, :] + looked_up.astype(jnp.float32)
    local_rows = local_in.reshape(-1, local_in.shape[-1])
    local_result, local_kept = layer_forward(
        local_rows, gains_here, layer_weights, lambda packed: codebook_forward(packed, head_count)
    )
    grad_rows, local_grads = layer_backward(
        local_rows,
        gains_here,
        layer_weights,
        local_kept,
        cotangent.astype(jnp.float32).reshape(local_rows.shape),
        lambda packed, grad_att, saved: codebook_backward(packed, grad_att, saved, head_count),
    )
    grad_frame = jnp.sum(grad_rows.reshape(local_in.shape), axis=2)
    table_slots = (books[None, None, :] * table.shape[1] + codes).reshape(-1)
    table_term = jax.ops.segment_sum(
        grad_rows, table_slots, num_segments=table.shape[0] * table.shape[1]
    ).reshape(table.shape)
    local_low = local_result.astype(jnp.bfloat16).reshape(cotangent.shape)
    table_part = jnp.where(on_first, jnp.zeros(table.shape, jnp.float32), table_term)
    grad_frame = jnp.where(on_first, jnp.zeros(frames.shape, jnp.float32), grad_frame)
    grad_table = lax.psum_scatter(table_part, ("section", "dp"), scatter_dimension=1, tiled=True)
    grad_back, local_copy = from_behind((grad_frame.astype(jnp.bfloat16), local_low), "section", -1)

    def global_back(totals, inputs):
        frame_rows, slot_lengths, grad_low = inputs
        doc_ends, (result, kept) = global_forward_rows(frame_rows, slot_lengths)
        grad_in, grads = layer_backward(
            frame_rows.astype(jnp.float32),
            gains_here,
            layer_weights,
            kept,
            grad_low.astype(jnp.float32),
            lambda packed, grad_att, saved: frame_backward(
                packed, grad_att, saved, query_pos, doc_ends, head_count
            ),
        )
        return (jax.tree.map(jnp.add, totals, grads), grad_in)

    global_grads, grad_frames = lax.scan(global_back, zero_grads, (frames, lengths, grad_back))

    def pick(global_part, local_part):
        return jnp.where(on_first, global_part, local_part)

    proj_sum, mix_sum, rise_sum, fall_sum, gain_sum = jax.tree.map(pick, global_grads, local_grads)
    proj_share, mix_share, rise_share, fall_share, gain_share = (
        lax.psum_scatter(proj_sum, "dp", scatter_dimension=0, tiled=True),
        lax.psum_scatter(mix_sum, "dp", scatter_dimension=1, tiled=True),
        lax.psum_scatter(rise_sum, "dp", scatter_dimension=0, tiled=True),
        lax.psum_scatter(fall_sum, "dp", scatter_dimension=1, tiled=True),
        lax.psum_scatter(gain_sum, "dp", scatter_dimension=1, tiled=True),
    )
    global_out = jnp.where(on_first, global_low, arrived)
    local_out = jnp.where(on_first, local_copy, local_low)
    input_grads = jnp.where(on_first, grad_frames, grad_frame)[None]
    return (
        global_out,
        local_out,
        input_grads,
        proj_share[None],
        mix_share[None],
        rise_share[None],
        fall_share[None],
        gain_share[None],
        grad_table,
    )


def lasting(us):
    return pl.CostEstimate(flops=int(us * 1.1e9), bytes_accessed=int(us * 1e6), transcendentals=0)

f32=jnp.float32; bf=jnp.bfloat16

def mm(a,b): return jnp.dot(a,b,preferred_element_type=f32)
def mm_nt(a,b): return lax.dot_general(a,b,(((1,),(1,)),((),())),preferred_element_type=f32)

def gelu_both(v):
    c0 = 0.7978845608028654
    c1 = c0 * 0.044715
    sq = v * v
    half = 0.5 + 0.5 * jnp.tanh(v * (c0 + c1 * sq))
    act = v * half
    return act, half + act * (1.0 - half) * (2.0 * c0 + 6.0 * c1 * sq)


def local_kernel(g_ref, emb_ref, cot_ref, gao_ref, gax_ref, gains_ref, e_ref, et_ref,
                 pqo, pqx, woo, wox, wuo, wux,
                 resid_o, acto_o, griso_o, gpo_o, actx_o, send_o, dx_o, gframe_o, gg_o,
                 q_s, k_s, v_s, p_s, gp_s, prod_s, wide_s, r_s, gm_s, gatt_s):
    F=g_ref.shape[0]; R=3*F; D=g_ref.shape[1]; H2=D//2
    W=acto_o.shape[2]
    grisx_o=send_o.at[:,:,0:W]
    mid_o,glow_o,normed_o=(send_o.at[:,:,W+j*D:W+(j+1)*D] for j in range(3))
    gpx_o=[send_o.at[:,:,W+3*D+j*H2:W+3*D+(j+1)*H2] for j in range(4)]
    step=pl.program_id(0)
    gain0=gains_ref[0:1,:]; gain1=gains_ref[1:2,:]
    g=g_ref[...].astype(f32)
    scr=(q_s,k_s,v_s)
    r0s=[]
    for c in range(3):
        x=g+emb_ref[c].astype(f32)
        r0=lax.rsqrt(jnp.mean(x*x,axis=-1,keepdims=True)+eps)
        r0s.append(r0)
        normed_o[c]=(x*r0*gain0).astype(bf)
    normed=normed_o[...].reshape(R,D)
    for j in range(3):
        scr[j][:,0:H2]=mm(normed,pqo[j]).astype(bf)
        scr[j][:,H2:D]=mm(normed,pqx[j]).astype(bf)
    pairs=[(c,c2) for c in range(3) for c2 in range(c+1)]
    rows=lambda ref,c: ref[c*F:(c+1)*F,:]
    for n,(c,c2) in enumerate(pairs):
        prod_s[n*F:(n+1)*F,:]=(rows(q_s,c).astype(f32)*rows(k_s,c2).astype(f32)).astype(bf)
    p_s[...]=mm(prod_s[...],e_ref[...])*0.125
    for c in range(3):
        own=[n for n,pr in enumerate(pairs) if pr[0]==c]
        ss=[rows(p_s,n) for n in own]
        top=functools.reduce(jnp.maximum,ss)
        ws=[jnp.exp(s-top) for s in ss]
        inv=1.0/functools.reduce(jnp.add,ws)
        for n,w in zip(own,ws): p_s[n*F:(n+1)*F,:]=w*inv
    wide_s[...]=mm(p_s[...].astype(bf),et_ref[...]).astype(bf)
    for c in range(3):
        acc=functools.reduce(jnp.add,[rows(wide_s,n).astype(f32)*rows(v_s,pr[1]).astype(f32) for n,pr in enumerate(pairs) if pr[0]==c])
        att=acc.astype(bf)
        gpo_o[0,c]=att[:,0:H2]; gpx_o[0][c]=att[:,H2:D]
    xs=(g_ref[...].astype(f32)[None]+emb_ref[...].astype(f32)).reshape(R,D)
    resid=xs+mm(gpo_o[0].reshape(R,H2),woo[...])+mm(gpx_o[0][...].reshape(R,H2),wox[...])
    r1=lax.rsqrt(jnp.mean(resid*resid,axis=-1,keepdims=True)+eps)
    resid_o[...]=resid.reshape(3,F,D)
    nm=(resid*r1*gain1).astype(bf)
    mid_o[...]=nm.reshape(3,F,D)
    ch=512
    gm=None
    for (wu,act_o,gris_o,ga_ref) in ((wuo,acto_o,griso_o,gao_ref),(wux,actx_o,grisx_o,gax_ref)):
        for j in range(wu.shape[1]//ch):
            sl=slice(j*ch,(j+1)*ch)
            w=wu[:,sl]
            act,gr=gelu_both(mm(nm,w))
            act_o[:,:,sl]=act.astype(bf).reshape(3,F,ch)
            gl=(ga_ref[:,:,sl].reshape(R,ch).astype(f32)*gr).astype(bf)
            gris_o[:,:,sl]=gl.reshape(3,F,ch)
            t=mm_nt(gl,w)
            if gm is None:
                gm_s[...]=t; gm=1
            else:
                gm_s[...]+=t
    gmid=gm_s[...]
    n1=resid_o[...].reshape(R,D)*r1
    u=gmid*gain1
    gres=cot_ref[...].reshape(R,D).astype(f32)+r1*(u-n1*jnp.mean(u*n1,axis=-1,keepdims=True))
    gsum1=jnp.sum(gmid*n1,axis=0,keepdims=True)
    r_s[...]=gres
    glow=gres.astype(bf)
    glow_o[...]=glow.reshape(3,F,D)
    gatt_s[:,0:H2]=mm_nt(glow,woo[...]).astype(bf)
    gatt_s[:,H2:D]=mm_nt(glow,wox[...]).astype(bf)
    def add(a,b): return b if a is None else a+b
    for n,(c,c2) in enumerate(pairs):
        prod_s[n*F:(n+1)*F,:]=(rows(gatt_s,c).astype(f32)*rows(v_s,c2).astype(f32)).astype(bf)
    gp_s[...]=mm(prod_s[...],e_ref[...])
    for c in range(3):
        own=[n for n,pr in enumerate(pairs) if pr[0]==c]
        ps=[rows(p_s,n) for n in own]
        gps=[rows(gp_s,n) for n in own]
        spread=functools.reduce(jnp.add,[p*gp for p,gp in zip(ps,gps)])
        for n,p,gp in zip(own,ps,gps): gp_s[n*F:(n+1)*F,:]=p*(gp-spread)*0.125
    prod_s[...]=mm(gp_s[...].astype(bf),et_ref[...]).astype(bf)
    for c in range(3):
        take=lambda which,left,right,at: functools.reduce(jnp.add,[rows(left,n).astype(f32)*rows(right,pr[1-which]).astype(f32) for n,pr in enumerate(pairs) if pr[which]==at]).astype(bf)
        for j,a in ((1,take(0,prod_s,k_s,c)),(2,take(1,prod_s,q_s,c)),(3,take(1,wide_s,gatt_s,c))):
            gpo_o[j,c]=a[:,0:H2]; gpx_o[j][c]=a[:,H2:D]
    gn=None
    for j in range(3):
        gn=add(gn,mm_nt(gpo_o[j+1].reshape(R,H2),pqo[j]))
        gn=gn+mm_nt(gpx_o[j+1][...].reshape(R,H2),pqx[j])
    gm_s[...]=gn
    tot=None; gsum0=None
    for c in range(3):
        gn=gm_s[c*F:(c+1)*F,:]
        n0=(g_ref[...].astype(f32)+emb_ref[c].astype(f32))*r0s[c]
        w=gn*gain0
        dx=r_s[c*F:(c+1)*F,:]+r0s[c]*(w-n0*jnp.mean(w*n0,axis=-1,keepdims=True))
        gsum0=add(gsum0,jnp.sum(gn*n0,axis=0,keepdims=True))
        dx_o[c]=dx.astype(bf)
        tot=add(tot,dx)
    gframe_o[...]=tot
    @pl.when(step==0)
    def _(): gg_o[...]=jnp.zeros_like(gg_o)
    gg_o[0:1,:]+=gsum0
    gg_o[1:2,:]+=gsum1

def local_skip(at_ref,*refs):
    @pl.when(at_ref[0]==1)
    def _():
        local_kernel(*refs)

def local_call(at,g,emb,cot,gao,gax,gains,pqo,pqx,woo,wox,wuo,wux,tile=128):
    N,D=g.shape; H2=D//2; FH=wuo.shape[1]; F=tile
    E=(jnp.arange(D)[:,None]//HEAD==jnp.arange(128)[None,:]).astype(bf)
    ET=E.T
    c3=lambda w: pl.BlockSpec((3,F,w),lambda i,s:(0,i,0))
    whole=lambda shp: pl.BlockSpec(shp,lambda i,s:(0,)*len(shp),pipeline_mode=pl.Buffered(1))
    sd=jax.ShapeDtypeStruct
    S=FH+3*D+4*H2
    out_shape=(sd((3,N,D),f32),sd((3,N,FH),bf),sd((3,N,FH),bf),sd((4,3,N,H2),bf),sd((3,N,FH),bf),sd((3,N,S),bf),sd((3,N,D),bf),sd((N,D),f32),sd((2,D),f32))
    gp=pl.BlockSpec((4,3,F,H2),lambda i,s:(0,0,i,0))
    return pl.pallas_call(local_skip, grid_spec=pltpu.PrefetchScalarGridSpec(num_scalar_prefetch=1,grid=(N//F,),
      in_specs=[pl.BlockSpec((F,D),lambda i,s:(i,0)),c3(D),c3(D),c3(FH),c3(FH),whole((2,D)),whole(E.shape),whole(ET.shape),
        whole(pqo.shape),whole(pqx.shape),whole(woo.shape),whole(wox.shape),whole(wuo.shape),whole(wux.shape)],
      out_specs=(c3(D),c3(FH),c3(FH),gp,c3(FH),c3(S),c3(D),pl.BlockSpec((F,D),lambda i,s:(i,0)),pl.BlockSpec((2,D),lambda i,s:(0,0))),
      scratch_shapes=[pltpu.VMEM((3*F,D),bf)]*3+[pltpu.VMEM((6*F,128),f32)]*2+[pltpu.VMEM((6*F,D),bf)]*2+[pltpu.VMEM((3*F,D),f32),pltpu.VMEM((3*F,D),f32),pltpu.VMEM((3*F,D),bf)]),
      out_shape=out_shape,
      compiler_params=pltpu.CompilerParams(vmem_limit_bytes=65400 * 1024),
      cost_estimate=lasting(57),
      name="local_layer",
    )(at,g,emb,cot,gao,gax,gains,E,ET,pqo,pqx,woo,wox,wuo,wux)

def attend_kernel(at_ref, xo_ref, xs_ref, xc_ref, xb_ref, gain_ref, proj_ref, qid_ref, kid_ref,
                  normed_ref, q_ref, k_ref, v_ref, near_ref, off_ref):
    step = pl.program_id(0)
    rows = xo_ref.shape[0]

    @pl.when((at_ref[0] == 0) & (step == 0))
    def _():
        for j, x_ref in enumerate((xo_ref, xs_ref, xc_ref, xb_ref)):
            part = slice(j * rows, (j + 1) * rows)
            x = x_ref[...].astype(f32)
            scale = lax.rsqrt(jnp.mean(x * x, axis=-1, keepdims=True) + eps)
            normed_ref[part, :] = (x * scale * gain_ref[0:1, :]).astype(bf)
        for j, ref in enumerate((q_ref, k_ref, v_ref)):
            ref[...] = mm(normed_ref[...], proj_ref[j]).astype(bf)

    @pl.when(at_ref[0] == 0)
    def _():
        bias = jnp.where(
            ((qid_ref[:, 1:2] == kid_ref[1:2, :]) & (kid_ref[0:1, :] <= qid_ref[:, 0:1]))
            | (kid_ref[0:1, :] == qid_ref[:, 0:1]),
            0.0,
            far,
        )
        lane = lax.broadcasted_iota(jnp.int32, (1, 2 * HEAD), 1) // HEAD
        here_rows = pl.ds(pl.multiple_of(step * rows, rows), rows)
        for pair in range(q_ref.shape[1] // (2 * HEAD)):
            cols = slice(pair * 2 * HEAD, (pair + 1) * 2 * HEAD)
            q, k, v = q_ref[here_rows, cols], k_ref[:, cols], v_ref[:, cols]
            total = None
            for side in range(2):
                here = lane == side
                scores = mm_nt(jnp.where(here, q * HEAD ** (-0.5), jnp.zeros_like(q)), k) + bias
                top = jnp.max(scores, axis=-1, keepdims=True)
                weights = jnp.exp(scores - top)
                mass = jnp.sum(weights, axis=-1, keepdims=True)
                probs = (weights * (1.0 / mass)).astype(bf)
                term = mm(probs, jnp.where(here, v, jnp.zeros_like(v)))
                total = term if total is None else total + term
            for odd, ref in ((0, near_ref), (1, off_ref)):

                @pl.when(step % 2 == odd)
                def _():
                    ref[0, :, cols] = total.astype(bf)


def attend_call(at, blocks, gains, proj, qid, kid):
    rows, width = blocks[0].shape
    cols = proj.shape[2] // 2
    total = 4 * rows
    whole = lambda shape: pl.BlockSpec(shape, lambda i, s: (0,) * len(shape))
    sd = jax.ShapeDtypeStruct
    half = pl.BlockSpec((1, rows, cols), lambda i, s: (i // 2, 0, 0))
    return pl.pallas_call(
        attend_kernel,
        grid_spec=pltpu.PrefetchScalarGridSpec(
            num_scalar_prefetch=1,
            grid=(4,),
            in_specs=[whole((rows, width))] * 4
            + [
                whole(gains.shape),
                pl.BlockSpec((3, width, cols), lambda i, s: (0, 0, s[2])),
                pl.BlockSpec((rows, 2), lambda i, s: (i, 0)),
                whole(kid.shape),
            ],
            out_specs=(whole((total, width)), *[whole((total, cols))] * 3, half, half),
        ),
        out_shape=(sd((total, width), bf), *[sd((total, cols), bf)] * 3, *[sd((2, rows, cols), bf)] * 2),
        compiler_params=pltpu.CompilerParams(vmem_limit_bytes=60 * 1024 * 1024),
        cost_estimate=lasting(18),
        name="frame_attention",
    )(at, *blocks, gains, proj, qid, kid)


def attend_back_kernel(at_ref, q_ref, k_ref, v_ref, g_ref, qid_ref, kid_ref, gq_ref, gk_ref, gv_ref, ks_ref, vs_ref):
    @pl.when(at_ref[0] == 0)
    def _():
        step = pl.program_id(0)

        @pl.when(step == 0)
        def _():
            ks_ref[...] = jnp.zeros_like(ks_ref)
            vs_ref[...] = jnp.zeros_like(vs_ref)

        bias = jnp.where(
            ((qid_ref[:, 1:2] == kid_ref[1:2, :]) & (kid_ref[0:1, :] <= qid_ref[:, 0:1]))
            | (kid_ref[0:1, :] == qid_ref[:, 0:1]),
            0.0,
            far,
        )
        lane = lax.broadcasted_iota(jnp.int32, (1, 2 * HEAD), 1) // HEAD
        for pair in range(q_ref.shape[1] // (2 * HEAD)):
            cols = slice(pair * 2 * HEAD, (pair + 1) * 2 * HEAD)
            q, k, v, g = q_ref[:, cols], k_ref[:, cols], v_ref[:, cols], g_ref[:, cols]
            gq = None
            for side in range(2):
                here = lane == side
                qh = jnp.where(here, q, jnp.zeros_like(q))
                gh = jnp.where(here, g, jnp.zeros_like(g))
                kh = jnp.where(here, k, jnp.zeros_like(k))
                scores = mm_nt(qh * HEAD ** (-0.5), k) + bias
                top = jnp.max(scores, axis=-1, keepdims=True)
                weights = jnp.exp(scores - top)
                mass = jnp.sum(weights, axis=-1, keepdims=True)
                probs = weights * (1.0 / mass)
                grad_probs = mm_nt(gh, v)
                spread = jnp.sum(probs * grad_probs, axis=-1, keepdims=True)
                gs = (probs * (grad_probs - spread) * HEAD ** (-0.5)).astype(bf)
                term = mm(gs, kh)
                gq = term if gq is None else gq + term
                ks_ref[:, cols] += across_rows(gs, qh)
                vs_ref[:, cols] += across_rows(probs.astype(bf), gh)
            gq_ref[:, cols] = gq.astype(bf)

        @pl.when(step == pl.num_programs(0) - 1)
        def _():
            gk_ref[...] = ks_ref[...].astype(bf)
            gv_ref[...] = vs_ref[...].astype(bf)


def attend_back_call(at, q, k, v, g, qid, kid, rows):
    total, width = q.shape
    part = pl.BlockSpec((rows, width), lambda i, s: (i, 0))
    whole = pl.BlockSpec((total, width), lambda i, s: (0, 0))
    shape = jax.ShapeDtypeStruct((total, width), bf)
    return pl.pallas_call(
        attend_back_kernel,
        grid_spec=pltpu.PrefetchScalarGridSpec(
            num_scalar_prefetch=1,
            grid=(total // rows,),
            in_specs=[part, whole, whole, part, pl.BlockSpec((rows, 2), lambda i, s: (i, 0)), pl.BlockSpec(kid.shape, lambda i, s: (0, 0))],
            out_specs=(part, whole, whole),
            scratch_shapes=[pltpu.VMEM((total, width), f32)] * 2,
        ),
        out_shape=(shape, shape, shape),
        compiler_params=pltpu.CompilerParams(vmem_limit_bytes=60 * 1024 * 1024),
        cost_estimate=lasting(0.01),
        name="frame_attention_back",
    )(at, q, k, v, g, qid, kid)


def front_kernel(at_ref, x_ref, near_ref, off_ref, core_ref, gain_ref, oo_ref, ox_ref, uo_ref, ux_ref, do_ref, dx_ref,
                 resid_ref, mid_ref, act_o, act_x, slope_o, slope_x, out_ref, total_ref):
    @pl.when(at_ref[0] == 0)
    def _():
        step = pl.program_id(0)
        turn = pl.num_programs(0) // 2

        @pl.when(step == 0)
        def _():
            cols = near_ref.shape[2]
            resid = x_ref[...].astype(f32)
            for flip, part, out in ((0, near_ref, oo_ref), (1, off_ref, oo_ref), (0, core_ref, ox_ref), (1, core_ref, ox_ref)):
                spot = pl.ds(pl.multiple_of((at_ref[2] ^ flip) * cols, cols), cols)
                resid = resid + mm(part[flip if part is core_ref else 0], out[spot, :])
            resid_ref[...] = resid
            scale = lax.rsqrt(jnp.mean(resid * resid, axis=-1, keepdims=True) + eps)
            mid_ref[...] = (resid * scale * gain_ref[1:2, :]).astype(bf)
            total_ref[...] = resid

        def part(up, down, act_ref, slope_ref):
            act, slope = gelu_both(mm(mid_ref[...], up[...]))
            act = act.astype(bf)
            act_ref[...] = act
            slope_ref[...] = slope.astype(bf)
            total_ref[...] += mm(act, down[...])

        @pl.when(step < turn)
        def _():
            part(uo_ref, do_ref, act_o, slope_o)

        @pl.when(step >= turn)
        def _():
            part(ux_ref, dx_ref, act_x, slope_x)

        @pl.when(step == pl.num_programs(0) - 1)
        def _():
            out_ref[...] = total_ref[...].astype(bf)


def halves_specs(turn, chunk, width, rows):
    first = lambda i, s: jnp.minimum(i, turn - 1) * (1 - s[0])
    later = lambda i, s: jnp.maximum(i - turn, 0) * (1 - s[0])
    ups = [pl.BlockSpec((width, chunk), lambda i, s, f=f: (0, f(i, s))) for f in (first, later)]
    downs = [pl.BlockSpec((chunk, width), lambda i, s, f=f: (f(i, s), 0)) for f in (first, later)]
    cols = [pl.BlockSpec((rows, chunk), lambda i, s, f=f: (0, f(i, s))) for f in (first, later)]
    return ups, downs, cols


def front_call(at, x, near, off, from_core, gains, out_own, out_oth, up_own, up_oth, down_own, down_oth, chunk=1024):
    rows, width = x.shape
    hidden = up_own.shape[1]
    turn = hidden // chunk
    ups, downs, cols = halves_specs(turn, chunk, width, rows)
    whole = lambda a: pl.BlockSpec(a.shape, lambda i, s: (0,) * a.ndim)
    sd = jax.ShapeDtypeStruct
    full = pl.BlockSpec((rows, width), lambda i, s: (0, 0))
    hid = sd((rows, hidden), bf)
    return pl.pallas_call(
        front_kernel,
        grid_spec=pltpu.PrefetchScalarGridSpec(
            num_scalar_prefetch=1,
            grid=(2 * turn,),
            in_specs=[full, whole(near), whole(off), whole(from_core), whole(gains), whole(out_own), whole(out_oth), *ups, *downs],
            out_specs=(full, full, cols[0], cols[1], cols[0], cols[1], full),
            scratch_shapes=[pltpu.VMEM((rows, width), f32)],
        ),
        out_shape=(sd((rows, width), f32), sd((rows, width), bf), hid, hid, hid, hid, sd((rows, width), bf)),
        compiler_params=pltpu.CompilerParams(vmem_limit_bytes=60 * 1024 * 1024),
        cost_estimate=lasting(15),
        name="global_forward",
    )(at, x, near, off, from_core, gains, out_own, out_oth, up_own, up_oth, down_own, down_oth)


def back_kernel(at_ref, g_ref, resid_ref, gain_ref, so_ref, sx_ref, uo_ref, ux_ref, do_ref, dx_ref,
                rise_o, rise_x, grad_ref, low_ref, gsum_ref, total_ref):
    @pl.when(at_ref[0] == 0)
    def _():
        step = pl.program_id(0)
        turn = pl.num_programs(0) // 2

        def part(up, down, slope_ref, rise_ref):
            rise = (mm_nt(g_ref[...], down[...]) * slope_ref[...].astype(f32)).astype(bf)
            rise_ref[...] = rise
            return mm_nt(rise, up[...])

        @pl.when(step == 0)
        def _():
            total_ref[...] = part(uo_ref, do_ref, so_ref, rise_o)

        @pl.when((step > 0) & (step < turn))
        def _():
            total_ref[...] += part(uo_ref, do_ref, so_ref, rise_o)

        @pl.when(step >= turn)
        def _():
            total_ref[...] += part(ux_ref, dx_ref, sx_ref, rise_x)

        @pl.when(step == pl.num_programs(0) - 1)
        def _():
            resid = resid_ref[...]
            scale = lax.rsqrt(jnp.mean(resid * resid, axis=-1, keepdims=True) + eps)
            normal = resid * scale
            total = total_ref[...]
            unit = total * gain_ref[1:2, :]
            grad = g_ref[...].astype(f32) + scale * (unit - normal * jnp.mean(unit * normal, axis=-1, keepdims=True))
            grad_ref[...] = grad
            low_ref[...] = grad.astype(bf)
            gsum_ref[...] = jnp.sum(total * normal, axis=0, keepdims=True)


def back_call(at, g, resid, gains, slope_own, slope_oth, up_own, up_oth, down_own, down_oth, chunk=1024):
    rows, width = g.shape
    hidden = up_own.shape[1]
    turn = hidden // chunk
    ups, downs, cols = halves_specs(turn, chunk, width, rows)
    sd = jax.ShapeDtypeStruct
    full = pl.BlockSpec((rows, width), lambda i, s: (0, 0))
    hid = sd((rows, hidden), bf)
    line = pl.BlockSpec((1, width), lambda i, s: (0, 0))
    return pl.pallas_call(
        back_kernel,
        grid_spec=pltpu.PrefetchScalarGridSpec(
            num_scalar_prefetch=1,
            grid=(2 * turn,),
            in_specs=[full, full, pl.BlockSpec(gains.shape, lambda i, s: (0, 0)), *cols, *ups, *downs],
            out_specs=(*cols, full, full, line),
            scratch_shapes=[pltpu.VMEM((rows, width), f32)],
        ),
        out_shape=(hid, hid, sd((rows, width), f32), sd((rows, width), bf), sd((1, width), f32)),
        compiler_params=pltpu.CompilerParams(vmem_limit_bytes=60 * 1024 * 1024),
        cost_estimate=lasting(13),
        name="global_backward",
    )(at, g, resid, gains, slope_own, slope_oth, up_own, up_oth, down_own, down_oth)


def split_sides(total, side, mine_ref, theirs_ref, at):
    half = total.shape[0] // 2
    top, bottom = total[:half].astype(bf), total[half:].astype(bf)
    mine_ref[at] = jnp.where(side == 0, top, bottom)
    theirs_ref[at] = jnp.where(side == 0, bottom, top)


def deal(total_ref, at_ref, mine_ref, theirs_ref, plane_first):
    piece = total_ref.shape[0] // 8
    for jz in range(4):
        for jy in range(2):
            place = (at_ref[1] ^ jz) * 2 + (at_ref[2] ^ jy)
            rows = pl.ds(pl.multiple_of(place * piece, piece), piece)
            low, high = jz % 2, jz // 2
            part = total_ref[rows, :].astype(bf)
            if plane_first:
                (theirs_ref if low else mine_ref)[high, jy] = part
            else:
                (theirs_ref if jy else mine_ref)[low * 2 + high] = part


def weight_kernel(at_ref, left, left_in, right, right_in, mine_ref, theirs_ref, total_ref, turned, turned_in, *, here, plane_first):
    @pl.when(at_ref[0] == here)
    def _():
        @pl.when(pl.program_id(0) == 0)
        def _():
            turned[...] = left[...].T
            turned_in[...] = left_in[...].T

        total_ref[...] = mm(turned[...], right[...]) + mm(turned_in[...], right_in[...])
        deal(total_ref, at_ref, mine_ref, theirs_ref, plane_first)


def weight_call(at, here, four, skip, plane_first, name, us, width, cols, chunk=512):
    piece = width // 8
    now = lambda i, s: jnp.where(s[0] == here, i, 0)
    whole = [
        pl.BlockSpec((a.shape[0], width), lambda i, s, c=c: (0, c), pipeline_mode=pl.Buffered(1))
        for a, c in zip(four[:2], skip)
    ]
    part = [
        pl.BlockSpec((a.shape[0], chunk), lambda i, s, c=c: (0, now(i, s) + c)) for a, c in zip(four[2:], skip[2:])
    ]
    if plane_first:
        shape = jax.ShapeDtypeStruct((2, 2, piece, cols), bf)
        out = pl.BlockSpec((2, 2, piece, chunk), lambda i, s: (0, 0, 0, now(i, s)))
    else:
        shape = jax.ShapeDtypeStruct((4, piece, cols), bf)
        out = pl.BlockSpec((4, piece, chunk), lambda i, s: (0, 0, now(i, s)))
    return pl.pallas_call(
        functools.partial(weight_kernel, here=here, plane_first=plane_first),
        grid_spec=pltpu.PrefetchScalarGridSpec(
            num_scalar_prefetch=1,
            grid=(cols // chunk,),
            in_specs=whole + part,
            out_specs=(out, out),
            scratch_shapes=[pltpu.VMEM((width, chunk), f32)] + [pltpu.VMEM((width, a.shape[0]), bf) for a in four[:2]],
        ),
        out_shape=(shape, shape),
        compiler_params=pltpu.CompilerParams(vmem_limit_bytes=60 * 1024 * 1024),
        cost_estimate=lasting(us),
        name=name,
    )(at, *four)


def rest_kernel(at_ref, *refs, here):
    pairs = (len(refs) - 3) // 4
    lows, normeds, rights = (refs[j * pairs : (j + 1) * pairs] for j in range(3))
    mine_ref, theirs_ref, total_ref = refs[3 * pairs : 3 * pairs + 3]
    turned = refs[3 * pairs + 3 :]
    step = pl.program_id(0)
    piece = total_ref.shape[0] // 8

    @pl.when(at_ref[0] == here)
    def _():
        for when, lefts in ((0, lows), (1, normeds)):

            @pl.when(step == when)
            def _():
                for left, turn in zip(lefts, turned):
                    turn[...] = left[...].T

        total = None
        for turn, right in zip(turned, rights):
            term = mm(turn[...], right[0] if len(right.shape) == 3 else right[...])
            total = term if total is None else total + term
        total_ref[...] = total
        for jz in range(4):
            for jy in range(2):
                place = (at_ref[1] ^ jz) * 2 + (at_ref[2] ^ jy)
                rows = pl.ds(pl.multiple_of(place * piece, piece), piece)
                for h in range(mine_ref.shape[2]):
                    cols = slice(h * mine_ref.shape[4], (h + 1) * mine_ref.shape[4])
                    (theirs_ref if jy else mine_ref)[jz % 2 * 2 + jz // 2, 0, h] = total_ref[rows, cols].astype(bf)


def rest_call(at, here, lows, normeds, rights, name, us, width):
    piece = width // 8
    count = 4
    narrow = width // 4
    size = rights[0][0].shape[2]
    whole = lambda pair: pl.BlockSpec((pair[0].shape[0], width), lambda i, s: (0, pair[1]), pipeline_mode=pl.Buffered(1))

    def part(pair):
        a, c = pair
        now = lambda i, s: jnp.where(s[0] == here, i, 0)
        if a.ndim == 3:
            return pl.BlockSpec((1,) + a.shape[1:], lambda i, s: (now(i, s), 0, 0))
        return pl.BlockSpec((a.shape[0], size), lambda i, s: (0, c + now(i, s)))

    halves = size // narrow
    shape = jax.ShapeDtypeStruct((4, count, halves, piece, narrow), bf)
    out = pl.BlockSpec((4, 1, halves, piece, narrow), lambda i, s: (0, jnp.where(s[0] == here, i, 0), 0, 0, 0))
    return pl.pallas_call(
        functools.partial(rest_kernel, here=here),
        grid_spec=pltpu.PrefetchScalarGridSpec(
            num_scalar_prefetch=1,
            grid=(count,),
            in_specs=[*map(whole, lows), *map(whole, normeds), *map(part, rights)],
            out_specs=(out, out),
            scratch_shapes=[pltpu.VMEM((width, size), f32)] + [pltpu.VMEM((width, a.shape[0]), bf) for a, _ in lows],
        ),
        out_shape=(shape, shape),
        compiler_params=pltpu.CompilerParams(vmem_limit_bytes=60 * 1024 * 1024),
        cost_estimate=lasting(us),
        name=name,
    )(at, *(a for a, _ in (*lows, *normeds, *rights)))


def fall_kernel(at_ref, resid_ref, ao_ref, ax_ref, do_ref, dx_ref, out_ref, total_ref):
    step = pl.program_id(0)
    turn = pl.num_programs(0) // 2
    books, planes, half = out_ref.shape[1], out_ref.shape[0], out_ref.shape[2]

    @pl.when(at_ref[0] == 1)
    def _():
        @pl.when(step == 0)
        def _():
            total_ref[...] = resid_ref[...]

        @pl.when(step < turn)
        def _():
            total_ref[...] += mm(ao_ref[...], do_ref[...])

        @pl.when(step >= turn)
        def _():
            total_ref[...] += mm(ax_ref[...], dx_ref[...])

        @pl.when(step == pl.num_programs(0) - 1)
        def _():
            for c in range(books):
                for z in range(planes):
                    first = (c * planes + z) * half
                    out_ref[z, c] = total_ref[first : first + half, :].astype(bf)


def fall_call(at, resid, act_own, act_oth, down_own, down_oth, planes, books, chunk=1024):
    rows, width = resid.shape
    turn = down_own.shape[0] // chunk
    first = lambda i, s: jnp.minimum(i, turn - 1) * s[0]
    later = lambda i, s: jnp.maximum(i - turn, 0) * s[0]
    col = lambda f: pl.BlockSpec((rows, chunk), lambda i, s: (0, f(i, s)))
    row = lambda f: pl.BlockSpec((chunk, width), lambda i, s: (f(i, s), 0))
    shape = (planes, books, rows // planes // books, width)
    return pl.pallas_call(
        fall_kernel,
        grid_spec=pltpu.PrefetchScalarGridSpec(
            num_scalar_prefetch=1,
            grid=(2 * turn,),
            in_specs=[pl.BlockSpec((rows, width), lambda i, s: (0, 0), pipeline_mode=pl.Buffered(1)), col(first), col(later), row(first), row(later)],
            out_specs=pl.BlockSpec(shape, lambda i, s: (0, 0, 0, 0)),
            scratch_shapes=[pltpu.VMEM((rows, width), f32)],
        ),
        out_shape=jax.ShapeDtypeStruct(shape, bf),
        compiler_params=pltpu.CompilerParams(vmem_limit_bytes=60 * 1024 * 1024),
        cost_estimate=lasting(0.01),
        name="local_output",
    )(at, resid, act_own, act_oth, down_own, down_oth)


def table_kernel(at_ref, code_ref, code_in_ref, own_ref, got_ref, low_ref, high_ref, total_ref):
    entries = total_ref.shape[0]
    slots = lax.broadcasted_iota(jnp.int32, (entries, code_ref.shape[2]), 0)
    piece = low_ref.shape[3]

    @pl.when(at_ref[0] == 1)
    def _():
        hot = (slots == code_ref[0]).astype(f32).astype(bf)
        hot_in = (slots == code_in_ref[0]).astype(f32).astype(bf)
        total_ref[...] = mm(hot, own_ref[0]) + mm(hot_in, got_ref[0])
        for jz in range(4):
            for jy in range(2):
                place = (at_ref[1] ^ jz) * 2 + (at_ref[2] ^ jy)
                spot = (jz % 2) * 2 + jz // 2
                for ref, base in ((low_ref, 0), (high_ref, entries // 2)):
                    rows = pl.ds(pl.multiple_of(base + place * piece, piece), piece)
                    ref[jy, spot, 0] = total_ref[rows, :].astype(bf)


def table_call(at, codes, codes_in, own, got, entries):
    books, rows = codes.shape
    width = own.shape[2]
    line = pl.BlockSpec((1, 1, rows), lambda c, s: (c, 0, 0))
    block = pl.BlockSpec((1, rows, width), lambda c, s: (c, 0, 0))
    shape = (2, 4, books, entries // 16, width)
    out = pl.BlockSpec((2, 4, 1, entries // 16, width), lambda c, s: (0, 0, c, 0, 0))
    return pl.pallas_call(
        table_kernel,
        grid_spec=pltpu.PrefetchScalarGridSpec(
            num_scalar_prefetch=1,
            grid=(books,),
            in_specs=[line, line, block, block],
            out_specs=(out, out),
            scratch_shapes=[pltpu.VMEM((entries, width), f32)],
        ),
        out_shape=(jax.ShapeDtypeStruct(shape, bf),) * 2,
        compiler_params=pltpu.CompilerParams(vmem_limit_bytes=60 * 1024 * 1024),
        cost_estimate=lasting(4),
        name="table_gradient",
    )(at, codes[:, None, :], codes_in[:, None, :], own, got)


def prepare_kernel(at_ref, code_ref, cot_ref, do_ref, dx_ref, table_ref, look_ref, po_ref, px_ref):
    step = pl.program_id(0)
    turn = pl.num_programs(0) // 2
    books, rows, chunk = po_ref.shape

    @pl.when(at_ref[0] == 1)
    def _():
        @pl.when(step < look_ref.shape[0])
        def _():
            slots = lax.broadcasted_iota(jnp.int32, (rows, table_ref.shape[1]), 1)
            hot = (slots == code_ref[jnp.minimum(step, look_ref.shape[0] - 1)]).astype(f32).astype(bf)
            look_ref[jnp.minimum(step, look_ref.shape[0] - 1)] = mm(hot, table_ref[0]).astype(bf)

        @pl.when(step < turn)
        def _():
            po_ref[...] = mm_nt(cot_ref[...], do_ref[...]).astype(bf).reshape(books, rows, chunk)

        @pl.when(step >= turn)
        def _():
            px_ref[...] = mm_nt(cot_ref[...], dx_ref[...]).astype(bf).reshape(books, rows, chunk)


def prepare_call(at, codes, cot, down_own, down_oth, table, chunk=512):
    books, rows = codes.shape
    width = cot.shape[1]
    hidden = down_own.shape[0]
    turn = hidden // chunk
    first = lambda i, s: jnp.minimum(i, turn - 1) * s[0]
    later = lambda i, s: jnp.maximum(i - turn, 0) * s[0]
    down = lambda f: pl.BlockSpec((chunk, width), lambda i, s: (f(i, s), 0))
    out = lambda f: pl.BlockSpec((books, rows, chunk), lambda i, s: (0, 0, f(i, s)))
    sd = jax.ShapeDtypeStruct
    return pl.pallas_call(
        prepare_kernel,
        grid_spec=pltpu.PrefetchScalarGridSpec(
            num_scalar_prefetch=1,
            grid=(2 * turn,),
            in_specs=[
                pl.BlockSpec((books, rows, 1), lambda i, s: (0, 0, 0)),
                pl.BlockSpec(cot.shape, lambda i, s: (0, 0)),
                down(first),
                down(later),
                pl.BlockSpec((1,) + table.shape[1:], lambda i, s: (jnp.minimum(i, books - 1) * s[0], 0, 0)),
            ],
            out_specs=(pl.BlockSpec((books, rows, width), lambda i, s: (0, 0, 0)), out(first), out(later)),
        ),
        out_shape=(sd((books, rows, width), bf), sd((books, rows, hidden), bf), sd((books, rows, hidden), bf)),
        compiler_params=pltpu.CompilerParams(vmem_limit_bytes=60 * 1024 * 1024),
        cost_estimate=lasting(5),
        name="local_prepare",
    )(at, codes[:, :, None], cot, down_own, down_oth, table)


def fence(*groups):
    return lax.optimization_barrier(groups)


def body(frames, codes, lengths, gains, w_qkv, w_out, w_up, w_down, table, cotangent):
    batches, share, width = frames.shape
    members = lax.axis_size("dp") // batches
    if (
        lax.axis_size("section") != 2
        or lax.axis_size("tensor") != 2
        or members != 2
        or lax.axis_size("dp") != 2 * batches
        or batches & (batches - 1)
        or share % 32
        or table.shape[1] != width
    ):
        return plain_body(frames, codes, lengths, gains, w_qkv, w_out, w_up, w_down, table, cotangent)
    place, core = lax.axis_index("dp"), lax.axis_index("tensor")
    plane, side = place // members, place % members
    on_first = lax.axis_index("section") == 0
    half = share // 2
    rows = batches * half
    count = 2 * batches
    at = jnp.stack([lax.axis_index("section"), plane, side]).astype(jnp.int32)

    everywhere, first, second = (0, 1), (0,), (1,)

    def linked(a, flip_place, flip_core, sections=everywhere):
        pairs = [
            ((z * count + i) * 2 + j, (z * count + (i ^ flip_place)) * 2 + (j ^ flip_core))
            for z in sections
            for i in range(count)
            for j in range(2)
        ]
        return lax.ppermute(a, ("section", "dp", "tensor"), pairs)

    def core_swap(a, sections=everywhere):
        return linked(a, 0, 1, sections)

    def side_swap(a, sections=everywhere):
        return linked(a, 1, 0, sections)

    def both_swap(a, sections=everywhere):
        return linked(a, 1, 1, sections)

    def to_local(a):
        return lax.ppermute(a, "section", [(0, 1)])

    def to_global(a):
        return lax.ppermute(a, "section", [(1, 0)])

    def planes_in(a, sections=everywhere):
        pieces = [lax.dynamic_slice_in_dim(a, plane ^ k, 1, 0) for k in range(batches)]
        return jnp.concatenate([pieces[0], *(linked(pieces[k], 2 * k, 0, sections) for k in range(1, batches))], 0)

    def planes_out(a, sections=everywhere):
        got = [a[:1], *(linked(a[k : k + 1], 2 * k, 0, sections) for k in range(1, batches))]
        out = jnp.zeros_like(a)
        for k in range(batches):
            out = lax.dynamic_update_slice_in_dim(out, got[k], plane ^ k, 0)
        return out

    def core_half(a, axis):
        return lax.dynamic_slice_in_dim(a, core * half, half, axis)

    def join_cores(a, axis):
        other = core_swap(a)
        return jnp.where(core == 0, jnp.concatenate([a, other], axis), jnp.concatenate([other, a], axis))

    def quarter(a, axis):
        size = a.shape[axis] // 2
        return lax.dynamic_slice_in_dim(a, side * size, size, axis)

    def by_side(mine, theirs, axis):
        return jnp.where(side == 0, jnp.concatenate([mine, theirs], axis), jnp.concatenate([theirs, mine], axis))

    x_own = planes_in(core_half(frames, 1), first).reshape(rows, width)
    x_side = side_swap(x_own, first)
    x_core, x_both = core_swap(x_own), core_swap(x_side)

    def positions(jt, js):
        base = ((jnp.arange(batches)[:, None] ^ plane) * 2 + (side ^ js)) * share + (core ^ jt) * half
        return (base + jnp.arange(half)[None, :]).reshape(-1)

    pos = jnp.concatenate([positions(0, 0), positions(0, 1), positions(1, 0), positions(1, 1)]).astype(jnp.int32)
    doc_ends = jnp.cumsum(lax.dynamic_index_in_dim(lengths, plane, 0, keepdims=False))
    doc = doc_index(pos, doc_ends)
    qid = jnp.stack([pos, doc], 1)
    kid = jnp.stack([pos, jnp.where(pos < doc_ends[-1], doc, -1)], 0)

    cot = planes_in(core_half(cotangent.transpose(0, 2, 1, 3), 2), second)
    codes_own = planes_in(core_half(codes.transpose(0, 2, 1), 2), second)
    (x_core, x_both, qid, kid, cot, codes_own), (w_qkv, w_out, w_up, w_down) = fence(
        (x_core, x_both, qid, kid, cot, codes_own), (w_qkv, w_out, w_up, w_down)
    )
    gains_here = gains[0]
    proj_own = w_qkv[0].transpose(1, 0, 2)
    out_own, up_own, down_own = w_out[0], w_up[0], w_down[0]
    out_oth, up_oth, down_oth = (core_swap(w) for w in (out_own, up_own, down_own))
    proj_oth = core_swap(proj_own)

    normed_all, q, k, v, near, off = attend_call(at, (x_own, x_side, x_core, x_both), gains_here, proj_own, qid, kid)
    proj_mine = quarter(proj_own, 2)
    off_got = side_swap(off, first)
    from_core = core_swap(jnp.concatenate([near[1:], off_got[1:]], 0))
    attended = jnp.stack([near[0], off[0], near[1], off[1]]).reshape(4 * rows, -1)
    x32 = x_own.astype(f32)
    resid, mid, act_own, act_oth, slope_own, slope_oth, global_low = front_call(
        at, x_own, near, off_got, from_core, gains_here, out_own, out_oth, up_own, up_oth, down_own, down_oth
    )
    mid_in, act_in = core_swap(mid), core_swap(act_oth)

    arrived = to_local(global_low)
    cot = cot.transpose(1, 0, 2, 3).reshape(CODEBOOKS, rows, width)
    codes_own = codes_own.transpose(1, 0, 2).reshape(CODEBOOKS, rows)
    slots = jnp.arange(table.shape[1], dtype=jnp.int32)
    cot_rows = cot.reshape(-1, width)
    cot_in, codes_oth = core_swap(cot_rows), core_swap(codes_own)

    looked_up, pull_own, pull_oth = prepare_call(at, codes_own, cot_rows, down_own, down_oth, table)
    (
        l_resid, l_act, l_rise, l_pack, l_act_oth, l_send, l_grad, l_frame, l_gains,
    ) = local_call(
        at, arrived, looked_up, cot, pull_own, pull_oth, gains_here, proj_own, proj_oth, out_own, out_oth, up_own, up_oth
    )
    global_moved = planes_out(global_low.reshape(batches, half, width), first)
    (l_frame, l_grad, l_act_oth, global_moved), (l_send,) = fence((l_frame, l_grad, l_act_oth, global_moved), (l_send,))
    grad_low = to_global(l_frame.astype(bf))

    flat = lambda a: a.reshape(-1, a.shape[-1])
    hidden = up_own.shape[1]

    def swap(a, bit, sections=everywhere):
        return linked(a, 1 << bit, 0, sections)

    def meet(mine, got):
        return (mine.astype(f32) + got.astype(f32)).astype(bf)

    def cols_of(a, which):
        return lax.dynamic_slice_in_dim(a, which * (width // 2), width // 2, 2)

    l_grad_in, l_act_in = core_swap(cols_of(l_grad, 1 - core)), core_swap(flat(l_act_oth), second)
    table_low, table_high = table_call(at, codes_own, codes_oth, cols_of(l_grad, core), l_grad_in, table.shape[1])
    l_down_mine, l_down_theirs = weight_call(
        at, 1, (cot_rows, cot_in, flat(l_act), l_act_in), (0, 0, 0, 0), True, "local_down_gradient", 4, width, hidden
    )
    (table_low, table_high, grad_low, l_down_theirs), (l_send,) = fence(
        (table_low, table_high, grad_low, l_down_theirs), (l_send,)
    )
    l_got = core_swap(flat(l_send), second)

    grad_in_low = core_swap(grad_low)
    rise_own, rise_oth, grad_resid, low_own, gain_mid = back_call(
        at, grad_low, resid, gains_here, slope_own, slope_oth, up_own, up_oth, down_own, down_oth
    )
    rise_in = core_swap(rise_oth)
    local_low = fall_call(at, flat(l_resid), flat(l_act), flat(l_act_oth), down_own, down_oth, batches, CODEBOOKS)
    (low_own, grad_in_low, local_low), (l_got,) = fence((low_own, grad_in_low, local_low), (l_got,))
    local_moved = planes_out(local_low, second)
    low_side = side_swap(low_own, first)
    down_mine, down_theirs = weight_call(
        at, 0, (grad_low, grad_in_low, act_own, act_in), (0, 0, 0, 0), True, "down_gradient", 8, width, hidden
    )
    l_up_mine, l_up_theirs = weight_call(
        at, 1, (flat(l_send), l_got, flat(l_rise), l_got),
        (hidden // width, hidden // width, 0, 0), False, "local_up_gradient", 4, width, hidden,
    )
    down_theirs = jnp.where(on_first, down_theirs, l_down_theirs)
    (down_theirs, l_up_theirs, local_moved), (rise_in, table_low) = fence(
        (down_theirs, l_up_theirs, local_moved), (rise_in, table_low)
    )
    table_moved = to_global(table_low)
    down_got = swap(down_theirs, 1)
    up_mine, up_theirs = weight_call(
        at, 0, (mid, mid_in, rise_own, rise_in), (0, 0, 0, 0), False, "up_gradient", 8, width, hidden
    )
    up_theirs = jnp.where(on_first, up_theirs, l_up_theirs)
    (up_theirs, low_side), (l_pack, l_act) = fence((up_theirs, low_side), (l_pack, l_act))
    up_got = swap(up_theirs, 0)
    low_at = hidden // width + 1
    l_rest_mine, l_rest_theirs = rest_call(
        at, 1, ((flat(l_send), low_at), (l_got, low_at)), ((flat(l_send), low_at + 1), (l_got, low_at + 1)),
        ((l_pack.reshape(4, CODEBOOKS * rows, -1), 0), (l_got, (hidden + 3 * width) // l_pack.shape[-1])),
        "local_rest_gradient", 0.01, width,
    )
    (l_rest_theirs, low_side), = fence((l_rest_theirs, low_side))
    low_all = jnp.concatenate([low_own, low_side, core_swap(low_own), core_swap(low_side)], 0)
    grad_att = against_rows(low_all, quarter(out_own, 0)).astype(bf)
    grad_packs = attend_back_call(at, q, k, v, grad_att, qid, kid, rows)
    rest_mine, rest_theirs = rest_call(
        at, 0, ((low_all, 0),), ((normed_all, 0),), ((jnp.stack([attended, *grad_packs]), 0),), "rest_gradient", 0.01, width
    )
    flip = side == 0
    empty = jnp.zeros_like(rest_mine)

    def spread_out(a):
        return jnp.concatenate([jnp.where(flip, a, empty), jnp.where(flip, empty, a)], 2)

    rest_theirs = jnp.where(on_first, spread_out(rest_theirs), l_rest_theirs)
    (rest_theirs, down_got, up_got), (grad_packs, rest_mine, local_moved) = fence(
        (rest_theirs, down_got, up_got), (grad_packs, rest_mine, local_moved)
    )
    rest_got = swap(rest_theirs, 0)
    rest_mine = jnp.where(on_first, spread_out(rest_mine), l_rest_mine)
    up_now = meet(jnp.where(on_first, up_mine, l_up_mine), up_got)
    up_got = swap(up_now[2:], 1)
    down_now = meet(jnp.where(on_first, down_mine, l_down_mine), down_got)
    down_got = swap(down_now[1], 2)
    part_normed = sum(against_rows(g, proj_mine[j]) for j, g in enumerate(grad_packs))
    pair = part_normed[: 2 * rows] + core_swap(part_normed[2 * rows :].astype(bf)).astype(f32)
    pair_side = side_swap(pair[rows:].astype(bf), first)
    local_sent = to_global(local_moved)
    (rest_got, rest_mine, up_got, down_got, pair_side, table_moved), = fence(
        (rest_got, rest_mine, up_got, down_got, pair_side, table_moved)
    )
    rest_now = meet(rest_mine, rest_got)
    (rest_now,), (up_got, down_got, pair_side) = fence((rest_now,), (up_got, down_got, pair_side))
    rest_got = swap(rest_now[2:], 1)
    down_now = meet(down_now[0], down_got)
    down_got = swap(down_now[1], 0)
    up_now = meet(up_now[:2], up_got)
    up_got = swap(up_now[1], 2)
    grad_normed = pair[:rows] + pair_side.astype(f32)
    back_in, gain_in = rms_back(x32, gains_here[0], grad_normed)
    grad_frames = grad_resid + back_in
    gain_sum = jnp.where(on_first, jnp.concatenate([gain_in[None], gain_mid]), l_gains)
    gain_sum = (gain_sum + core_swap(gain_sum)).reshape(2, batches, 2, -1)
    piece = width // count
    gain_rows = jnp.concatenate(
        [
            lax.dynamic_slice(gain_sum, (0, plane ^ (2 * j + i), side ^ y, 0), (2, 1, 1, piece)).reshape(1, -1)
            for y in range(2)
            for i in range(2)
            for j in range(2)
        ]
    ).reshape(2, batches, 2 * piece)
    gain_rows = jnp.pad(gain_rows.astype(bf)[:, :, None, :], ((0, 0), (0, 0), (0, 15), (0, width // 2 - 2 * piece)))
    table_now = jnp.where(on_first, table_moved, table_high).reshape(2, batches, -1, width // 2)
    table_now = jnp.concatenate([table_now, gain_rows], 2)
    table_got = swap(table_now[1], 0)
    inner = jnp.where(on_first, grad_frames, l_frame).astype(bf).reshape(2, 2, half, width)
    inner_got = swap(inner[1], 2)
    (rest_got, up_got, down_got, table_got, local_sent, inner_got), (global_moved,) = fence(
        (rest_got, up_got, down_got, table_got, local_sent, inner_got), (global_moved,)
    )
    rest_now = meet(rest_now[:2], rest_got)
    rest_got = swap(rest_now[1], 2)
    table_now = meet(table_now[0], table_got)
    table_got = swap(table_now[2:], 1)
    near_got = swap(jnp.stack([inner[0, 1], inner_got[1]]), 1)
    global_sent = to_local(global_moved)
    local_out = join_cores(jnp.where(on_first, local_sent, local_moved), 2).transpose(0, 2, 1, 3)
    (near_got, rest_got, global_sent, local_out), = fence((near_got, rest_got, global_sent, local_out))
    blocks = (inner[0, 0], near_got[0], inner_got[0], near_got[1])
    inner = jnp.zeros((batches, half, width), bf)
    for k, block in enumerate(blocks):
        inner = lax.dynamic_update_slice_in_dim(inner, block[None], plane ^ k, 0)
    global_out = join_cores(jnp.where(on_first, global_moved, global_sent), 1)
    down_share = down_now[0].astype(f32) + down_got.astype(f32)
    up_share = up_now[0].astype(f32) + up_got.astype(f32)
    table_now = meet(table_now[:2], table_got)
    table_got = swap(table_now[1], 2)
    input_grads = join_cores(inner, 1).astype(f32)[None]
    mix = out_own.shape[0]
    (local_out, global_out, up_share, down_share), (rest_got, table_got) = fence(
        (local_out, global_out, up_share, down_share.T), (rest_got, table_got)
    )
    rest_share = rest_now[0].astype(f32) + rest_got.astype(f32)
    table_now = table_now[0].astype(f32) + table_got.astype(f32)
    gain_share = table_now[-16, : 2 * piece].reshape(2, piece)
    grad_table = join_cores(table_now[:-16].reshape(CODEBOOKS, -1, width // 2).astype(bf), 2).astype(f32)

    mix = out_own.shape[0]
    proj_share = rest_share[1:].transpose(2, 0, 1, 3).reshape(piece, 3, mix)
    return (
        global_out,
        local_out,
        input_grads,
        proj_share[None],
        rest_share[0].transpose(0, 2, 1).reshape(mix, piece)[None],
        up_share[None],
        down_share[None],
        gain_share[None],
        grad_table,
    )


def solution(mesh):
    in_specs = (
        P(None, "dp", None),
        P(None, "dp", None),
        P(),
        P("section", None, None),
        P("section", None, None, "tensor"),
        P("section", "tensor", None),
        P("section", None, "tensor"),
        P("section", "tensor", None),
        P(),
        P(None, "dp", None, None),
    )
    out_specs = (
        P(None, "dp", None),
        P(None, "dp", None, None),
        P("section", None, "dp", None),
        P("section", "dp", None, "tensor"),
        P("section", "tensor", "dp"),
        P("section", "dp", "tensor"),
        P("section", "tensor", "dp"),
        P("section", None, "dp"),
        P(None, ("section", "dp"), None),
    )
    return jax.shard_map(body, mesh=mesh, in_specs=in_specs, out_specs=out_specs, check_vma=False)
```

profile of v0, /device:TPU:3, one launch (start us, length us, event | category | flops | bytes accessed | tf_op | source)
XLA Modules:
  0.0 471.1 jit_solution(8844383496385132466)
XLA Ops:
  5.9 5.2 %collective-permute-start.8 = (bf16[1,3,64,1024]{3,2,1,0:T(8,128)(2,1)S(1)}, bf16[1,3,64,1024]{3,2,1,0:T(8,128)(2,1)S(1)}, u32[]{:S(2)}, u32[]{:S(2)}) collective-permute-start(bf16[1,3,64,1024]{3,2,1,0:T(8,128)(2,1)S(1)} %get-tuple-element.283), channel_id=1, source_target_pairs={{16,28},{17,29},{18,30},{19,31},{20,24},{21,25},{22,26},{23,27},{2... | collective-permute-start | bytes 1179656 | tf_op jit(solution)/shard_map/ppermute | solution.py:1072
  16.4 5.0 %collective-permute-start.9 = (s32[1,3,64]{2,0,1:T(1,128)S(1)}, s32[1,3,64]{2,0,1:T(1,128)S(1)}, u32[]{:S(2)}, u32[]{:S(2)}) collective-permute-start(s32[1,3,64]{2,0,1:T(1,128)S(1)} %get-tuple-element.307), channel_id=1, source_target_pairs={{16,20},{17,21},{18,22},{19,23},{20,16},{21,17},{22,18},{23,19},{2... | collective-permute-start | bytes 2312 | tf_op jit(solution)/shard_map/ppermute | solution.py:1072
  24.6 5.8 %collective-permute-start.7 = (bf16[1,3,64,1024]{3,2,1,0:T(8,128)(2,1)S(1)}, bf16[1,3,64,1024]{3,2,1,0:T(8,128)(2,1)S(1)}, u32[]{:S(2)}, u32[]{:S(2)}) collective-permute-start(bf16[1,3,64,1024]{3,2,1,0:T(8,128)(2,1)S(1)} %get-tuple-element.284), channel_id=1, source_target_pairs={{16,24},{17,25},{18,26},{19,27},{20,28},{21,29},{22,30},{23,31},{2... | collective-permute-start | bytes 1179656 | tf_op jit(solution)/shard_map/ppermute | solution.py:1072
  35.8 11.2 %collective-permute-done.7 = bf16[1,3,64,1024]{3,2,1,0:T(8,128)(2,1)S(1)} collective-permute-done((bf16[1,3,64,1024]{3,2,1,0:T(8,128)(2,1)S(1)}, bf16[1,3,64,1024]{3,2,1,0:T(8,128)(2,1)S(1)}, u32[]{:S(2)}, u32[]{:S(2)}) %collective-permute-start.7) | collective-permute-done | bytes 393248 | tf_op jit(solution)/shard_map/ppermute | solution.py:1072
  54.9 5.8 %frame_attention.1 = (bf16[1024,1024]{1,0:T(8,128)(2,1)}, bf16[1024,256]{1,0:T(8,128)(2,1)}, bf16[1024,256]{1,0:T(8,128)(2,1)}, bf16[1024,256]{1,0:T(8,128)(2,1)...) custom-call(s32[3]{0:T(128)} %pad_add_fusion.3.at_ref, bf16[256,1024]{1,0:T(8,128)(2,1)} %bitcast.176, ...), custom_call_target="tpu_custom_call" | custom-call | flops 19800000512 | bytes 18000000 | tf_op jit(solution)/shard_map/frame_attention/pallas_call | solution.py:540
  69.6 7.2 %global_forward.1 = (f32[256,1024]{1,0:T(8,128)}, bf16[256,1024]{1,0:T(8,128)(2,1)}, bf16[256,2048]{1,0:T(8,128)(2,1)}, bf16[256,2048]{1,0:T(8,128)(2,1)}, bf16[...) custom-call(s32[3]{0:T(128)} %pad_add_fusion.3.at_ref, bf16[256,1024]{1,0:T(8,128)(2,1)} %bitcast.177, ...), custom_call_target="tpu_custom_call" | custom-call | flops 16499999744 | bytes 15000000 | tf_op jit(solution)/shard_map/global_forward/pallas_call | solution.py:685
  81.2 17.1 %local_prepare.1 = (bf16[3,256,1024]{2,1,0:T(8,128)(2,1)}, bf16[3,256,2048]{2,1,0:T(8,128)(2,1)}, bf16[3,256,2048]{2,1,0:T(8,128)(2,1)}) custom-call(s32[3]{0:T(128)} %pad_add_fusion.3.at_ref, s32[3,256,1]{2,1,0:T(8,128)} %broadcast_in_dim_reshape.16.code_ref, bf16[768,1024]{1,0:T(8,128)(2,1)} %bitcast.199, bf16[2048,1024]{1,0:T(8,128)(2,1)} %bitcast.181, ...), custom_call_target="tpu_custom_call" | custom-call | flops 5500000256 | bytes 5000000 | tf_op jit(solution)/shard_map/local_prepare/pallas_call | solution.py:1017
  105.9 54.7 %local_layer.1 = (f32[3,256,1024]{2,1,0:T(8,128)}, bf16[3,256,2048]{2,1,0:T(8,128)(2,1)}, bf16[3,256,2048]{2,1,0:T(8,128)(2,1)}, bf16[4,3,256,512]{3,2,1,0:T(8,1...) custom-call(s32[3]{0:T(128)} %pad_add_fusion.3.at_ref, ...), custom_call_target="tpu_custom_call" | custom-call | flops 62699999232 | bytes 57000000 | tf_op jit(solution)/shard_map/local_layer/pallas_call | solution.py:477
  171.9 5.8 %table_gradient.1 = (bf16[2,4,3,64,512]{4,3,2,1,0:T(8,128)(2,1)}, bf16[2,4,3,64,512]{4,3,2,1,0:T(8,128)(2,1)}) custom-call(s32[3]{0:T(128)} %pad_add_fusion.3.at_ref, s32[3,1,256]{2,1,0:T(1,128)} %broadcast_in_dim_reshape.12.code_ref, s32[3,1,256]{2,1,0:T(1,128)} %broadcast_in_dim.17.code_in_ref, bf16[3,256,512]{2,1,0:T(8,128)(2,1)} %get-tuple-element.290.own_ref, ...), custom_call_target="tpu_custom_call" | custom-call | flops 4400000000 | bytes 4000000 | tf_op jit(solution)/shard_map/table_gradient/pallas_call | solution.py:969
  178.9 12.9 %local_down_gradient.1 = (bf16[2,2,128,2048]{3,2,1,0:T(8,128)(2,1)}, bf16[2,2,128,2048]{3,2,1,0:T(8,128)(2,1)}) custom-call(s32[3]{0:T(128)} %pad_add_fusion.3.at_ref, bf16[768,1024]{1,0:T(8,128)(2,1)} %bitcast.202, bf16[768,1024]{1,0:T(8,128)(2,1)} %copy-done.41, bf16[768,2048]{1,0:T(8,128)(2,1)} %bitcast.188, ...), custom_call_target="tpu_custom_call" | custom-call | flops 4400000000 | bytes 4000000 | tf_op jit(solution)/shard_map/local_down_gradient/pallas_call | solution.py:812
  194.7 13.8 %local_output.1 = bf16[4,3,64,1024]{3,2,1,0:T(8,128)(2,1)} custom-call(s32[3]{0:T(128)} %pad_add_fusion.3.at_ref, f32[768,1024]{1,0:T(8,128)} %bitcast.187, bf16[768,2048]{1,0:T(8,128)(2,1)} %bitcast.189, bf16[768,2048]{1,0:T(8,128)(2,1)} %bitcast.191, bf16[2048,1024]{1,0:T(8,128)(2,1)} %bitcast.182, bf16[2048,1024]{1,0:T(8,128)(2,1)} %collective-permute-done.17.dx_ref), custom_call_target="tpu_custom_call" | custom-call | flops 11000000 | bytes 10000 | tf_op jit(solution)/shard_map/local_output/pallas_call | solution.py:927
  208.6 6.3 %global_backward.1 = (bf16[256,2048]{1,0:T(8,128)(2,1)}, bf16[256,2048]{1,0:T(8,128)(2,1)}, f32[256,1024]{1,0:T(8,128)}, bf16[256,1024]{1,0:T(8,128)(2,1)}, f32[1,1024]{1,0:T(1,128)}) custom-call(s32[3]{0:T(128)} %pad_add_fusion.3.at_ref, bf16[256,1024]{1,0:T(8,128)(2,1)} %copy-done.45, f32[256,1024]{1,0:T(8,128)} %get-tuple-element.154.resid_ref, ...), custom_call_target="tpu_custom_call" | custom-call | flops 14300000256 | bytes 13000000 | tf_op jit(solution)/shard_map/global_backward/pallas_call | solution.py:747
  219.7 4.7 collective-permute-start.32
  232.4 12.7 %local_up_gradient.1 = (bf16[4,128,2048]{2,1,0:T(8,128)(2,1)}, bf16[4,128,2048]{2,1,0:T(8,128)(2,1)}) custom-call(s32[3]{0:T(128)} %pad_add_fusion.3.at_ref, bf16[768,7168]{1,0:T(8,128)(2,1)} %bitcast.169, bf16[768,7168]{1,0:T(8,128)(2,1)} %collective-permute-done.28.left_in.right_in.refs_1_.refs_3_.refs_5_, bf16[768,2048]{1,0:T(8,128)(2,1)} %bitcast.185, ...), custom_call_target="tpu_custom_call" | custom-call | flops 4400000000 | bytes 4000000 | tf_op jit(solution)/shard_map/local_up_gradient/pallas_call | solution.py:812
  251.5 7.9 %collective-permute-start.38 = (bf16[2,2,128,2048]{3,2,1,0:T(8,128)(2,1)S(1)}, bf16[2,2,128,2048]{3,2,1,0:T(8,128)(2,1)}, u32[]{:S(2)}, u32[]{:S(2)}) collective-permute-start(bf16[2,2,128,2048]{3,2,1,0:T(8,128)(2,1)S(1)} %broadcast_select_fusion), channel_id=1, source_target_pairs={{0,4},{1,5},{2,6},{3,7},{4,0},{5,1},{6,2},{7,3},{8,12},{9,13},{10,... | collective-permute-start | bytes 6291464 | tf_op jit(solution)/shard_map/ppermute | solution.py:1072
  269.8 14.5 %local_rest_gradient.1 = (bf16[4,4,2,128,256]{4,3,2,1,0:T(8,128)(2,1)}, bf16[4,4,2,128,256]{4,3,2,1,0:T(8,128)(2,1)}) custom-call(s32[3]{0:T(128)} %pad_add_fusion.3.at_ref, bf16[768,7168]{1,0:T(8,128)(2,1)} %bitcast.170, bf16[768,7168]{1,0:T(8,128)(2,1)} %collective-permute-done.28.left_in.right_in.refs_1_.refs_3_.refs_5_, bf16[768,7168]{1,0:T(8,128)(2,1)} %bitcast.171, ...), custom_call_target="tpu_custom_call" | custom-call | flops 11000000 | bytes 10000 | tf_op jit(solution)/shard_map/local_rest_gradient/pallas_call | solution.py:876
  293.4 4.9 %frame_attention_back.1 = (bf16[1024,256]{1,0:T(8,128)(2,1)}, bf16[1024,256]{1,0:T(8,128)(2,1)}, bf16[1024,256]{1,0:T(8,128)(2,1)}) custom-call(s32[3]{0:T(128)} %pad_add_fusion.3.at_ref, bf16[1024,256]{1,0:T(8,128)(2,1)} %get-tuple-element.184.q_ref, bf16[1024,256]{1,0:T(8,128)(2,1)} %get-tuple-element.185.k_ref, ...), custom_call_target="tpu_custom_call" | custom-call | flops 11000000 | bytes 10000 | tf_op jit(solution)/shard_map/frame_attention_back/pallas_call | solution.py:612
  301.3 4.0 rest_gradient.1
  335.7 14.3 %collective-permute-done.42 = bf16[2,128,2048]{2,1,0:T(8,128)(2,1)} collective-permute-done((bf16[2,128,2048]{2,1,0:T(8,128)(2,1)}, bf16[2,128,2048]{2,1,0:T(8,128)(2,1)}, u32[]{:S(2)}, u32[]{:S(2)}) %collective-permute-start.42) | collective-permute-done | bytes 1048608 | tf_op jit(solution)/shard_map/ppermute | solution.py:1072
  350.0 22.8 %collective-permute-done.43 = bf16[2,128,2048]{2,1,0:T(8,128)(2,1)} collective-permute-done((bf16[2,128,2048]{2,1,0:T(8,128)(2,1)}, bf16[2,128,2048]{2,1,0:T(8,128)(2,1)}, u32[]{:S(2)}, u32[]{:S(2)}) %collective-permute-start.43) | collective-permute-done | bytes 1048608 | tf_op jit(solution)/shard_map/ppermute | solution.py:1072
  384.5 4.7 collective-permute-start.49
  395.7 24.1 %collective-permute-done.52 = bf16[2,64,1024]{2,1,0:T(8,128)(2,1)S(1)} collective-permute-done((bf16[2,64,1024]{2,1,0:T(8,128)(2,1)S(1)}, bf16[2,64,1024]{2,1,0:T(8,128)(2,1)S(1)}, u32[]{:S(2)}, u32[]{:S(2)}) %collective-permute-start.52) | collective-permute-done | bytes 262176 | tf_op jit(solution)/shard_map/ppermute | solution.py:1072
  431.3 16.8 %collective-permute-done.58 = bf16[2,208,512]{2,1,0:T(8,128)(2,1)S(1)} collective-permute-done((bf16[2,208,512]{2,1,0:T(8,128)(2,1)S(1)}, bf16[2,208,512]{2,1,0:T(8,128)(2,1)S(1)}, u32[]{:S(2)}, u32[]{:S(2)}) %collective-permute-start.58) | collective-permute-done | bytes 426016 | tf_op jit(solution)/shard_map/ppermute | solution.py:1072
  455.8 4.4 collective-permute-done.59
  (353 shorter events, 182.2 us)
Async XLA Ops:
  5.9 29.9 %collective-permute-start.8 = (bf16[1,3,64,1024]{3,2,1,0:T(8,128)(2,1)S(1)}, bf16[1,3,64,1024]{3,2,1,0:T(8,128)(2,1)S(1)}, u32[]{:S(2)}, u32[]{:S(2)}) collective-permute-start(bf16[1,3,64,1024]{3,2,1,0:T(8,128)(2,1)S(1)} %get-tuple-element.283), channel_id=1, source_target_pairs={{16,28},{17,29},{18,30},{19,31},{20,24},{21,25},{22,26},{23,27},{2... | collective-permute-start | bytes 1179656 | tf_op jit(solution)/shard_map/ppermute | solution.py:1072
  61.5 41.3 %collective-permute-start.19 = (bf16[3,1024,512]{2,1,0:T(8,128)(2,1)}, bf16[3,1024,512]{2,1,0:T(8,128)(2,1)}, u32[]{:S(2)}, u32[]{:S(2)}) collective-permute-start(bf16[3,1024,512]{2,1,0:T(8,128)(2,1)} %bitcast.205), channel_id=1, source_target_pairs={{0,1},{1,0},{2,3},{3,2},{4,5},{5,4},{6,7},{7,6},{8,9},{9,8},{10,11... | collective-permute-start | bytes 9437192 | tf_op jit(solution)/shard_map/ppermute | solution.py:1072
  76.8 29.0 %collective-permute-start.18 = (bf16[256,1024]{1,0:T(8,128)(2,1)}, bf16[256,1024]{1,0:T(8,128)(2,1)}, u32[]{:S(2)}, u32[]{:S(2)}) collective-permute-start(bf16[256,1024]{1,0:T(8,128)(2,1)} %get-tuple-element.136), channel_id=1, source_target_pairs={{0,16},{1,17},{2,18},{3,19},{4,20},{5,21},{6,22},{7,23},{8,24},{9,... | collective-permute-start | bytes 1572872 | tf_op jit(solution)/shard_map/ppermute | solution.py:1084
  194.1 65.3 %collective-permute-start.29 = (bf16[256,1024]{1,0:T(8,128)(2,1)}, bf16[256,1024]{1,0:T(8,128)(2,1)}, u32[]{:S(2)}, u32[]{:S(2)}) collective-permute-start(bf16[256,1024]{1,0:T(8,128)(2,1)} %get-tuple-element.163.left), channel_id=1, source_target_pairs={{0,1},{1,0},{2,3},{3,2},{4,5},{5,4},{6,7},{7,6},{8,9},{9,8},{10,11... | collective-permute-start | bytes 1572872 | tf_op jit(solution)/shard_map/ppermute | solution.py:1072
  194.3 30.1 %collective-permute-start.30 = (bf16[256,2048]{1,0:T(8,128)(2,1)}, bf16[256,2048]{1,0:T(8,128)(2,1)S(1)}, u32[]{:S(2)}, u32[]{:S(2)}) collective-permute-start(bf16[256,2048]{1,0:T(8,128)(2,1)} %get-tuple-element.167), channel_id=1, source_target_pairs={{0,1},{1,0},{2,3},{3,2},{4,5},{5,4},{6,7},{7,6},{8,9},{9,8},{10,11... | collective-permute-start | bytes 3145736 | tf_op jit(solution)/shard_map/ppermute | solution.py:1072
  215.0 36.5 %collective-permute-start.34 = (bf16[256,2048]{1,0:T(8,128)(2,1)}, bf16[256,2048]{1,0:T(8,128)(2,1)}, u32[]{:S(2)}, u32[]{:S(2)}) collective-permute-start(bf16[256,2048]{1,0:T(8,128)(2,1)} %get-tuple-element.173), channel_id=1, source_target_pairs={{0,1},{1,0},{2,3},{3,2},{4,5},{5,4},{6,7},{7,6},{8,9},{9,8},{10,11... | collective-permute-start | bytes 3145736 | tf_op jit(solution)/shard_map/ppermute | solution.py:1072
  217.8 27.3 %collective-permute-start.31 = (bf16[1,3,64,1024]{3,2,1,0:T(8,128)(2,1)}, bf16[1,3,64,1024]{3,2,1,0:T(8,128)(2,1)S(1)}, u32[]{:S(2)}, u32[]{:S(2)}) collective-permute-start(bf16[1,3,64,1024]{3,2,1,0:T(8,128)(2,1)} %get-tuple-element.287), channel_id=1, source_target_pairs={{16,20},{17,21},{18,22},{19,23},{20,16},{21,17},{22,18},{23,19},{2... | collective-permute-start | bytes 1179656 | tf_op jit(solution)/shard_map/ppermute | solution.py:1072
  219.7 30.2 %collective-permute-start.32 = (bf16[1,3,64,1024]{3,2,1,0:T(8,128)(2,1)S(1)}, bf16[1,3,64,1024]{3,2,1,0:T(8,128)(2,1)S(1)}, u32[]{:S(2)}, u32[]{:S(2)}) collective-permute-start(bf16[1,3,64,1024]{3,2,1,0:T(8,128)(2,1)S(1)} %get-tuple-element.286), channel_id=1, source_target_pairs={{16,24},{17,25},{18,26},{19,27},{20,28},{21,29},{22,30},{23,31},{2... | collective-permute-start | bytes 1179656 | tf_op jit(solution)/shard_map/ppermute | solution.py:1072
  224.4 26.3 %collective-permute-start.33 = (bf16[1,3,64,1024]{3,2,1,0:T(8,128)(2,1)S(1)}, bf16[1,3,64,1024]{3,2,1,0:T(8,128)(2,1)S(1)}, u32[]{:S(2)}, u32[]{:S(2)}) collective-permute-start(bf16[1,3,64,1024]{3,2,1,0:T(8,128)(2,1)S(1)} %get-tuple-element.285), channel_id=1, source_target_pairs={{16,28},{17,29},{18,30},{19,31},{20,24},{21,25},{22,26},{23,27},{2... | collective-permute-start | bytes 1179656 | tf_op jit(solution)/shard_map/ppermute | solution.py:1072
  251.5 57.4 %collective-permute-start.38 = (bf16[2,2,128,2048]{3,2,1,0:T(8,128)(2,1)S(1)}, bf16[2,2,128,2048]{3,2,1,0:T(8,128)(2,1)}, u32[]{:S(2)}, u32[]{:S(2)}) collective-permute-start(bf16[2,2,128,2048]{3,2,1,0:T(8,128)(2,1)S(1)} %broadcast_select_fusion), channel_id=1, source_target_pairs={{0,4},{1,5},{2,6},{3,7},{4,0},{5,1},{6,2},{7,3},{8,12},{9,13},{10,... | collective-permute-start | bytes 6291464 | tf_op jit(solution)/shard_map/ppermute | solution.py:1072
  265.6 45.7 %collective-permute-start.39 = (bf16[4,128,2048]{2,1,0:T(8,128)(2,1)}, bf16[4,128,2048]{2,1,0:T(8,128)(2,1)}, u32[]{:S(2)}, u32[]{:S(2)}) collective-permute-start(bf16[4,128,2048]{2,1,0:T(8,128)(2,1)} %broadcast_select_fusion.1), channel_id=1, source_target_pairs={{0,2},{1,3},{2,0},{3,1},{4,6},{5,7},{6,4},{7,5},{8,10},{9,11},{10,... | collective-permute-start | bytes 6291464 | tf_op jit(solution)/shard_map/ppermute | solution.py:1072
  287.1 46.2 %collective-permute-start.45 = (bf16[2,4,3,64,512]{4,3,2,1,0:T(8,128)(2,1)}, bf16[2,4,3,64,512]{4,3,2,1,0:T(8,128)(2,1)}, u32[]{:S(2)}, u32[]{:S(2)}) collective-permute-start(bf16[2,4,3,64,512]{4,3,2,1,0:T(8,128)(2,1)} %get-tuple-element.208), channel_id=1, source_target_pairs={{16,0},{17,1},{18,2},{19,3},{20,4},{21,5},{22,6},{23,7},{24,8},{25... | collective-permute-start | bytes 4718600 | tf_op jit(solution)/shard_map/ppermute | solution.py:1087
  311.4 61.4 %collective-permute-start.41 = (bf16[4,4,2,128,256]{4,3,2,1,0:T(8,128)(2,1)}, bf16[4,4,2,128,256]{4,3,2,1,0:T(8,128)(2,1)}, u32[]{:S(2)}, u32[]{:S(2)}) collective-permute-start(bf16[4,4,2,128,256]{4,3,2,1,0:T(8,128)(2,1)} %maximum_select_fusion.1), channel_id=1, source_target_pairs={{0,2},{1,3},{2,0},{3,1},{4,6},{5,7},{6,4},{7,5},{8,10},{9,11},{10,... | collective-permute-start | bytes 6291464 | tf_op jit(solution)/shard_map/ppermute | solution.py:1072
  316.4 33.7 %collective-permute-start.42 = (bf16[2,128,2048]{2,1,0:T(8,128)(2,1)}, bf16[2,128,2048]{2,1,0:T(8,128)(2,1)}, u32[]{:S(2)}, u32[]{:S(2)}) collective-permute-start(bf16[2,128,2048]{2,1,0:T(8,128)(2,1)} %slice.235), channel_id=1, source_target_pairs={{0,4},{1,5},{2,6},{3,7},{4,0},{5,1},{6,2},{7,3},{8,12},{9,13},{10,... | collective-permute-start | bytes 3145736 | tf_op jit(solution)/shard_map/ppermute | solution.py:1072
  327.3 45.5 %collective-permute-start.43 = (bf16[2,128,2048]{2,1,0:T(8,128)(2,1)}, bf16[2,128,2048]{2,1,0:T(8,128)(2,1)}, u32[]{:S(2)}, u32[]{:S(2)}) collective-permute-start(bf16[2,128,2048]{2,1,0:T(8,128)(2,1)} %slice_bitcast_fusion.1), channel_id=1, source_target_pairs={{0,8},{1,9},{2,10},{3,11},{4,12},{5,13},{6,14},{7,15},{8,0},{9,1},... | collective-permute-start | bytes 3145736 | tf_op jit(solution)/shard_map/ppermute | solution.py:1072
  331.5 41.3 %collective-permute-start.44 = (bf16[256,1024]{1,0:T(8,128)(2,1)S(1)}, bf16[256,1024]{1,0:T(8,128)(2,1)S(1)}, u32[]{:S(2)}, u32[]{:S(2)}) collective-permute-start(bf16[256,1024]{1,0:T(8,128)(2,1)S(1)} %slice.320), channel_id=1, source_target_pairs={{0,2},{1,3},{2,0},{3,1},{4,6},{5,7},{6,4},{7,5},{8,10},{9,11},{10,... | collective-permute-start | bytes 1572872 | tf_op jit(solution)/shard_map/ppermute | solution.py:1072
  333.3 60.9 %collective-permute-start.51 = (bf16[4,3,64,1024]{3,2,1,0:T(8,128)(2,1)}, bf16[4,3,64,1024]{3,2,1,0:T(8,128)(2,1)}, u32[]{:S(2)}, u32[]{:S(2)}) collective-permute-start(bf16[4,3,64,1024]{3,2,1,0:T(8,128)(2,1)} %constant_dynamic-update-slice_fusion.5), channel_id=1, source_target_pairs={{16,0},{17,1},{18,2},{19,3},{20,4},{21,5},{22,6},{23,7},{24,8},{25... | collective-permute-start | bytes 4718600 | tf_op jit(solution)/shard_map/ppermute | solution.py:1087
  376.2 43.7 %collective-permute-start.46 = (bf16[2,4,2,128,256]{4,3,2,1,0:T(8,128)(2,1)}, bf16[2,4,2,128,256]{4,3,2,1,0:T(8,128)(2,1)}, u32[]{:S(2)}, u32[]{:S(2)}) collective-permute-start(bf16[2,4,2,128,256]{4,3,2,1,0:T(8,128)(2,1)} %slice.201), channel_id=1, source_target_pairs={{0,4},{1,5},{2,6},{3,7},{4,0},{5,1},{6,2},{7,3},{8,12},{9,13},{10,... | collective-permute-start | bytes 3145736 | tf_op jit(solution)/shard_map/ppermute | solution.py:1072
  380.3 39.6 %collective-permute-start.47 = (bf16[128,2048]{1,0:T(8,128)(2,1)}, bf16[128,2048]{1,0:T(8,128)(2,1)}, u32[]{:S(2)}, u32[]{:S(2)}) collective-permute-start(bf16[128,2048]{1,0:T(8,128)(2,1)} %slice_bitcast_fusion.10), channel_id=1, source_target_pairs={{0,8},{1,9},{2,10},{3,11},{4,12},{5,13},{6,14},{7,15},{8,0},{9,1},... | collective-permute-start | bytes 1572872 | tf_op jit(solution)/shard_map/ppermute | solution.py:1072
  383.7 36.2 %collective-permute-start.48 = (bf16[128,2048]{1,0:T(8,128)(2,1)}, bf16[128,2048]{1,0:T(8,128)(2,1)}, u32[]{:S(2)}, u32[]{:S(2)}) collective-permute-start(bf16[128,2048]{1,0:T(8,128)(2,1)} %slice_bitcast_fusion.9), channel_id=1, source_target_pairs={{0,2},{1,3},{2,0},{3,1},{4,6},{5,7},{6,4},{7,5},{8,10},{9,11},{10,... | collective-permute-start | bytes 1572872 | tf_op jit(solution)/shard_map/ppermute | solution.py:1072
  392.4 27.4 %collective-permute-start.50 = (bf16[4,208,512]{2,1,0:T(8,128)(2,1)S(1)}, bf16[4,208,512]{2,1,0:T(8,128)(2,1)S(1)}, u32[]{:S(2)}, u32[]{:S(2)}) collective-permute-start(bf16[4,208,512]{2,1,0:T(8,128)(2,1)S(1)} %slice_bitcast_fusion.3), channel_id=1, source_target_pairs={{0,2},{1,3},{2,0},{3,1},{4,6},{5,7},{6,4},{7,5},{8,10},{9,11},{10,... | collective-permute-start | bytes 2555912 | tf_op jit(solution)/shard_map/ppermute | solution.py:1072
  419.9 31.5 %collective-permute-start.53 = (bf16[2,64,1024]{2,1,0:T(8,128)(2,1)S(1)}, bf16[2,64,1024]{2,1,0:T(8,128)(2,1)S(1)}, u32[]{:S(2)}, u32[]{:S(2)}) collective-permute-start(bf16[2,64,1024]{2,1,0:T(8,128)(2,1)S(1)} %pad_maximum_fusion.5), channel_id=1, source_target_pairs={{0,4},{1,5},{2,6},{3,7},{4,0},{5,1},{6,2},{7,3},{8,12},{9,13},{10,... | collective-permute-start | bytes 786440 | tf_op jit(solution)/shard_map/ppermute | solution.py:1072
  421.6 29.8 %collective-permute-start.54 = (bf16[4,2,128,256]{3,2,1,0:T(8,128)(2,1)S(1)}, bf16[4,2,128,256]{3,2,1,0:T(8,128)(2,1)S(1)}, u32[]{:S(2)}, u32[]{:S(2)}) collective-permute-start(bf16[4,2,128,256]{3,2,1,0:T(8,128)(2,1)S(1)} %slice_bitcast_fusion.8), channel_id=1, source_target_pairs={{0,8},{1,9},{2,10},{3,11},{4,12},{5,13},{6,14},{7,15},{8,0},{9,1},... | collective-permute-start | bytes 1572872 | tf_op jit(solution)/shard_map/ppermute | solution.py:1072
  423.1 28.3 %collective-permute-start.55 = (bf16[4,64,1024]{2,1,0:T(8,128)(2,1)}, bf16[4,64,1024]{2,1,0:T(8,128)(2,1)S(1)}, u32[]{:S(2)}, u32[]{:S(2)}) collective-permute-start(bf16[4,64,1024]{2,1,0:T(8,128)(2,1)} %constant_dynamic-update-slice_fusion.8), channel_id=1, source_target_pairs={{0,16},{1,17},{2,18},{3,19},{4,20},{5,21},{6,22},{7,23},{8,24},{9,... | collective-permute-start | bytes 1572872 | tf_op jit(solution)/shard_map/ppermute | solution.py:1084
  (88 other events, 808.2 us)
where the time goes:
time: 479 us; the launch traced here: 471 us
  Pallas kernels  166 us (35%)
  waiting for transfers between devices  106 us (22%)
  starting transfers between devices  93.9 us (20%)
  other arithmetic  51.1 us (11%)
  local copies, waits for them, and re-layouts  47.6 us (10%)
    ppermute x57, waiting for transfers between devices, linked(): return lax.ppermute(a, ('section', 'dp', 'tensor'), pairs)  103 us
    ppermute x57, starting transfers between devices, linked(): return lax.ppermute(a, ('section', 'dp', 'tensor'), pairs)  85.1 us
    pallas_call x1, Pallas kernels, local_call(): pl.pallas_call(local_skip, grid_spec=pltpu.PrefetchScalarGridSpec(num_sca...  54.7 us
    pallas_call x4, Pallas kernels, weight_call(): pl.pallas_call(functools.partial(weight_kernel, here=here, plane_first=pl...  32.1 us
    pallas_call x2, Pallas kernels, rest_call(): pl.pallas_call(functools.partial(rest_kernel, here=here), grid_spec=pltpu...  18.6 us
    pallas_call x1, Pallas kernels, prepare_call(): pl.pallas_call(prepare_kernel, grid_spec=pltpu.PrefetchScalarGridSpec(num...  17.1 us
    unnamed x108, local copies, waits for them, and re-layouts  14.3 us
    pallas_call x1, Pallas kernels, fall_call(): pl.pallas_call(fall_kernel, grid_spec=pltpu.PrefetchScalarGridSpec(num_sc...  13.8 us
  transfers between devices with their start and end apart: 62, of which 12 were waited for; matrix products, arithmetic and copies ran while one was open for 19% of the time, Pallas kernels for 24%

commit v1 on v0

--- a/solution.py
+++ b/solution.py
@@ -1155,13 +1155,17 @@
     cot_in, codes_oth = core_swap(cot_rows), core_swap(codes_own)
 
     looked_up, pull_own, pull_oth = prepare_call(at, codes_own, cot_rows, down_own, down_oth, table)
+    (pull_own, codes_oth, cot_in), = fence((pull_own, codes_oth, cot_in))
     (
         l_resid, l_act, l_rise, l_pack, l_act_oth, l_send, l_grad, l_frame, l_gains,
     ) = local_call(
         at, arrived, looked_up, cot, pull_own, pull_oth, gains_here, proj_own, proj_oth, out_own, out_oth, up_own, up_oth
     )
     global_moved = planes_out(global_low.reshape(batches, half, width), first)
-    (l_frame, l_grad, l_act_oth, global_moved), (l_send,) = fence((l_frame, l_grad, l_act_oth, global_moved), (l_send,))
+    global_sent = to_local(global_moved)
+    (l_frame, l_grad, l_act_oth, global_moved, global_sent), (l_send,) = fence(
+        (l_frame, l_grad, l_act_oth, global_moved, global_sent), (l_send,)
+    )
     grad_low = to_global(l_frame.astype(bf))
 
     flat = lambda a: a.reshape(-1, a.shape[-1])
@@ -1277,17 +1281,17 @@
     table_got = swap(table_now[1], 0)
     inner = jnp.where(on_first, grad_frames, l_frame).astype(bf).reshape(2, 2, half, width)
     inner_got = swap(inner[1], 2)
-    (rest_got, up_got, down_got, table_got, local_sent, inner_got), (global_moved,) = fence(
-        (rest_got, up_got, down_got, table_got, local_sent, inner_got), (global_moved,)
+    (rest_got, up_got, down_got, table_got, local_sent, inner_got), = fence(
+        (rest_got, up_got, down_got, table_got, local_sent, inner_got)
     )
     rest_now = meet(rest_now[:2], rest_got)
+    table_now = meet(table_now[0], table_got)
+    (table_now, rest_now), (inner_got, local_sent) = fence((table_now, rest_now), (inner_got, local_sent))
+    table_got = swap(table_now[2:], 1)
     rest_got = swap(rest_now[1], 2)
-    table_now = meet(table_now[0], table_got)
-    table_got = swap(table_now[2:], 1)
     near_got = swap(jnp.stack([inner[0, 1], inner_got[1]]), 1)
-    global_sent = to_local(global_moved)
     local_out = join_cores(jnp.where(on_first, local_sent, local_moved), 2).transpose(0, 2, 1, 3)
-    (near_got, rest_got, global_sent, local_out), = fence((near_got, rest_got, global_sent, local_out))
+    (near_got, rest_got, table_got, local_out), = fence((near_got, rest_got, table_got, local_out))
     blocks = (inner[0, 0], near_got[0], inner_got[0], near_got[1])
     inner = jnp.zeros((batches, half, width), bf)
     for k, block in enumerate(blocks):
@@ -1299,22 +1303,22 @@
     table_got = swap(table_now[1], 2)
     input_grads = join_cores(inner, 1).astype(f32)[None]
     mix = out_own.shape[0]
-    (local_out, global_out, up_share, down_share), (rest_got, table_got) = fence(
-        (local_out, global_out, up_share, down_share.T), (rest_got, table_got)
-    )
     rest_share = rest_now[0].astype(f32) + rest_got.astype(f32)
+    proj_share = rest_share[1:].transpose(2, 0, 1, 3).reshape(piece, 3, mix)
+    out_share = rest_share[0].transpose(0, 2, 1).reshape(mix, piece)
+    (local_out, global_out, up_share, down_share, input_grads, proj_share, out_share), (table_got,) = fence(
+        (local_out, global_out, up_share, down_share.T, input_grads, proj_share, out_share), (table_got,)
+    )
     table_now = table_now[0].astype(f32) + table_got.astype(f32)
     gain_share = table_now[-16, : 2 * piece].reshape(2, piece)
     grad_table = join_cores(table_now[:-16].reshape(CODEBOOKS, -1, width // 2).astype(bf), 2).astype(f32)
 
-    mix = out_own.shape[0]
-    proj_share = rest_share[1:].transpose(2, 0, 1, 3).reshape(piece, 3, mix)
     return (
         global_out,
         local_out,
         input_grads,
         proj_share[None],
-        rest_share[0].transpose(0, 2, 1).reshape(mix, piece)[None],
+        out_share[None],
         up_share[None],
         down_share[None],
         gain_share[None],

time: 479 us -> 476 us (level)
  waiting for transfers between devices: 106 us -> 114 us
  other arithmetic: 51.1 us -> 44.6 us
    ppermute x57, waiting for transfers between devices: 103 us -> 113 us  [linked(): return lax.ppermute(a, ('section', 'dp', 'tensor'), pairs)]
  transfers between devices with their start and end apart: 62 -> 62, of which waited for: 12 -> 12; matrix products, arithmetic and copies ran while one was open for 19% -> 17% of each run, Pallas kernels for 24% -> 36%
where the time goes in v1:
time: 476 us; the launch traced here: 468 us
  Pallas kernels  166 us (35%)
  waiting for transfers between devices  114 us (24%)
  starting transfers between devices  94.1 us (20%)
  other arithmetic  44.6 us (9%)
  local copies, waits for them, and re-layouts  43.2 us (9%)
    ppermute x57, waiting for transfers between devices, linked(): return lax.ppermute(a, ('section', 'dp', 'tensor'), pairs)  113 us
    ppermute x57, starting transfers between devices, linked(): return lax.ppermute(a, ('section', 'dp', 'tensor'), pairs)  85.3 us
    pallas_call x1, Pallas kernels, local_call(): pl.pallas_call(local_skip, grid_spec=pltpu.PrefetchScalarGridSpec(num_sca...  54.6 us
    pallas_call x4, Pallas kernels, weight_call(): pl.pallas_call(functools.partial(weight_kernel, here=here, plane_first=pl...  32.1 us
    pallas_call x2, Pallas kernels, rest_call(): pl.pallas_call(functools.partial(rest_kernel, here=here), grid_spec=pltpu...  18.6 us
    pallas_call x1, Pallas kernels, prepare_call(): pl.pallas_call(prepare_kernel, grid_spec=pltpu.PrefetchScalarGridSpec(num...  17.1 us
    pallas_call x1, Pallas kernels, fall_call(): pl.pallas_call(fall_kernel, grid_spec=pltpu.PrefetchScalarGridSpec(num_sc...  13.8 us
    unnamed x108, local copies, waits for them, and re-layouts  11.8 us
  transfers between devices with their start and end apart: 62, of which 12 were waited for; matrix products, arithmetic and copies ran while one was open for 17% of the time, Pallas kernels for 36%

profile of v1, /device:TPU:3, one launch (start us, length us, event | category | flops | bytes accessed | tf_op | source)
XLA Modules:
  0.0 467.8 jit_solution(8759475458463128438)
XLA Ops:
  5.9 5.2 %collective-permute-start.8 = (bf16[1,3,64,1024]{3,2,1,0:T(8,128)(2,1)S(1)}, bf16[1,3,64,1024]{3,2,1,0:T(8,128)(2,1)S(1)}, u32[]{:S(2)}, u32[]{:S(2)}) collective-permute-start(bf16[1,3,64,1024]{3,2,1,0:T(8,128)(2,1)S(1)} %get-tuple-element.301), channel_id=1, source_target_pairs={{16,28},{17,29},{18,30},{19,31},{20,24},{21,25},{22,26},{23,27},{2... | collective-permute-start | bytes 1179656 | tf_op jit(solution)/shard_map/ppermute | solution.py:1072
  16.4 5.0 %collective-permute-start.9 = (s32[1,3,64]{2,0,1:T(1,128)S(1)}, s32[1,3,64]{2,0,1:T(1,128)S(1)}, u32[]{:S(2)}, u32[]{:S(2)}) collective-permute-start(s32[1,3,64]{2,0,1:T(1,128)S(1)} %get-tuple-element.325), channel_id=1, source_target_pairs={{16,20},{17,21},{18,22},{19,23},{20,16},{21,17},{22,18},{23,19},{2... | collective-permute-start | bytes 2312 | tf_op jit(solution)/shard_map/ppermute | solution.py:1072
  24.1 6.3 %collective-permute-start.7 = (bf16[1,3,64,1024]{3,2,1,0:T(8,128)(2,1)S(1)}, bf16[1,3,64,1024]{3,2,1,0:T(8,128)(2,1)S(1)}, u32[]{:S(2)}, u32[]{:S(2)}) collective-permute-start(bf16[1,3,64,1024]{3,2,1,0:T(8,128)(2,1)S(1)} %get-tuple-element.302), channel_id=1, source_target_pairs={{16,24},{17,25},{18,26},{19,27},{20,28},{21,29},{22,30},{23,31},{2... | collective-permute-start | bytes 1179656 | tf_op jit(solution)/shard_map/ppermute | solution.py:1072
  35.8 11.2 %collective-permute-done.7 = bf16[1,3,64,1024]{3,2,1,0:T(8,128)(2,1)S(1)} collective-permute-done((bf16[1,3,64,1024]{3,2,1,0:T(8,128)(2,1)S(1)}, bf16[1,3,64,1024]{3,2,1,0:T(8,128)(2,1)S(1)}, u32[]{:S(2)}, u32[]{:S(2)}) %collective-permute-start.7) | collective-permute-done | bytes 393248 | tf_op jit(solution)/shard_map/ppermute | solution.py:1072
  54.8 5.8 %frame_attention.1 = (bf16[1024,1024]{1,0:T(8,128)(2,1)}, bf16[1024,256]{1,0:T(8,128)(2,1)}, bf16[1024,256]{1,0:T(8,128)(2,1)}, bf16[1024,256]{1,0:T(8,128)(2,1)...) custom-call(s32[3]{0:T(128)} %pad_add_fusion.3.at_ref, bf16[256,1024]{1,0:T(8,128)(2,1)} %bitcast.176, ...), custom_call_target="tpu_custom_call" | custom-call | flops 19800000512 | bytes 18000000 | tf_op jit(solution)/shard_map/frame_attention/pallas_call | solution.py:540
  69.7 7.2 %global_forward.1 = (f32[256,1024]{1,0:T(8,128)}, bf16[256,1024]{1,0:T(8,128)(2,1)}, bf16[256,2048]{1,0:T(8,128)(2,1)}, bf16[256,2048]{1,0:T(8,128)(2,1)}, bf16[...) custom-call(s32[3]{0:T(128)} %pad_add_fusion.3.at_ref, bf16[256,1024]{1,0:T(8,128)(2,1)} %bitcast.177, ...), custom_call_target="tpu_custom_call" | custom-call | flops 16499999744 | bytes 15000000 | tf_op jit(solution)/shard_map/global_forward/pallas_call | solution.py:685
  80.0 17.1 %local_prepare.1 = (bf16[3,256,1024]{2,1,0:T(8,128)(2,1)}, bf16[3,256,2048]{2,1,0:T(8,128)(2,1)}, bf16[3,256,2048]{2,1,0:T(8,128)(2,1)}) custom-call(s32[3]{0:T(128)} %pad_add_fusion.3.at_ref, s32[3,256,1]{2,1,0:T(8,128)} %broadcast_in_dim_reshape.8.code_ref, bf16[768,1024]{1,0:T(8,128)(2,1)} %bitcast.20.cot_ref.left, bf16[2048,1024]{1,0:T(8,128)(2,1)} %bitcast.181, ...), custom_call_target="tpu_custom_call" | custom-call | flops 5500000256 | bytes 5000000 | tf_op jit(solution)/shard_map/local_prepare/pallas_call | solution.py:1017
  105.0 54.6 %local_layer.1 = (f32[3,256,1024]{2,1,0:T(8,128)}, bf16[3,256,2048]{2,1,0:T(8,128)(2,1)}, bf16[3,256,2048]{2,1,0:T(8,128)(2,1)}, bf16[4,3,256,512]{3,2,1,0:T(8,1...) custom-call(s32[3]{0:T(128)} %pad_add_fusion.3.at_ref, ...), custom_call_target="tpu_custom_call" | custom-call | flops 62699999232 | bytes 57000000 | tf_op jit(solution)/shard_map/local_layer/pallas_call | solution.py:477
  169.9 5.8 %table_gradient.1 = (bf16[2,4,3,64,512]{4,3,2,1,0:T(8,128)(2,1)}, bf16[2,4,3,64,512]{4,3,2,1,0:T(8,128)(2,1)}) custom-call(s32[3]{0:T(128)} %pad_add_fusion.3.at_ref, s32[3,1,256]{2,1,0:T(1,128)} %broadcast_in_dim_reshape.6.code_ref, s32[3,1,256]{2,1,0:T(1,128)} %broadcast_in_dim.21.code_in_ref, bf16[3,256,512]{2,1,0:T(8,128)(2,1)} %get-tuple-element.308.own_ref, ...), custom_call_target="tpu_custom_call" | custom-call | flops 4400000000 | bytes 4000000 | tf_op jit(solution)/shard_map/table_gradient/pallas_call | solution.py:969
  175.7 12.9 %local_down_gradient.1 = (bf16[2,2,128,2048]{3,2,1,0:T(8,128)(2,1)}, bf16[2,2,128,2048]{3,2,1,0:T(8,128)(2,1)}) custom-call(s32[3]{0:T(128)} %pad_add_fusion.3.at_ref, bf16[768,1024]{1,0:T(8,128)(2,1)} %bitcast.20.cot_ref.left, bf16[768,1024]{1,0:T(8,128)(2,1)} %copy-done.40, bf16[768,2048]{1,0:T(8,128)(2,1)} %bitcast.188, ...), custom_call_target="tpu_custom_call" | custom-call | flops 4400000000 | bytes 4000000 | tf_op jit(solution)/shard_map/local_down_gradient/pallas_call | solution.py:812
  191.6 13.8 %local_output.1 = bf16[4,3,64,1024]{3,2,1,0:T(8,128)(2,1)} custom-call(s32[3]{0:T(128)} %pad_add_fusion.3.at_ref, f32[768,1024]{1,0:T(8,128)} %bitcast.187, bf16[768,2048]{1,0:T(8,128)(2,1)} %bitcast.189, bf16[768,2048]{1,0:T(8,128)(2,1)} %bitcast.191, bf16[2048,1024]{1,0:T(8,128)(2,1)} %bitcast.182, bf16[2048,1024]{1,0:T(8,128)(2,1)} %collective-permute-done.12.dx_ref), custom_call_target="tpu_custom_call" | custom-call | flops 11000000 | bytes 10000 | tf_op jit(solution)/shard_map/local_output/pallas_call | solution.py:927
  205.5 6.4 %global_backward.1 = (bf16[256,2048]{1,0:T(8,128)(2,1)}, bf16[256,2048]{1,0:T(8,128)(2,1)}, f32[256,1024]{1,0:T(8,128)}, bf16[256,1024]{1,0:T(8,128)(2,1)}, f32[1,1024]{1,0:T(1,128)}) custom-call(s32[3]{0:T(128)} %pad_add_fusion.3.at_ref, bf16[256,1024]{1,0:T(8,128)(2,1)} %copy-done.45, f32[256,1024]{1,0:T(8,128)} %get-tuple-element.166.resid_ref, ...), custom_call_target="tpu_custom_call" | custom-call | flops 14300000256 | bytes 13000000 | tf_op jit(solution)/shard_map/global_backward/pallas_call | solution.py:747
  216.7 4.7 collective-permute-start.33
  229.3 12.7 %local_up_gradient.1 = (bf16[4,128,2048]{2,1,0:T(8,128)(2,1)}, bf16[4,128,2048]{2,1,0:T(8,128)(2,1)}) custom-call(s32[3]{0:T(128)} %pad_add_fusion.3.at_ref, bf16[768,7168]{1,0:T(8,128)(2,1)} %bitcast.169, bf16[768,7168]{1,0:T(8,128)(2,1)} %collective-permute-done.29.left_in.right_in.refs_1_.refs_3_.refs_5_, bf16[768,2048]{1,0:T(8,128)(2,1)} %bitcast.185, ...), custom_call_target="tpu_custom_call" | custom-call | flops 4400000000 | bytes 4000000 | tf_op jit(solution)/shard_map/local_up_gradient/pallas_call | solution.py:812
  248.4 7.9 %collective-permute-start.39 = (bf16[2,2,128,2048]{3,2,1,0:T(8,128)(2,1)S(1)}, bf16[2,2,128,2048]{3,2,1,0:T(8,128)(2,1)}, u32[]{:S(2)}, u32[]{:S(2)}) collective-permute-start(bf16[2,2,128,2048]{3,2,1,0:T(8,128)(2,1)S(1)} %broadcast_select_fusion), channel_id=1, source_target_pairs={{0,4},{1,5},{2,6},{3,7},{4,0},{5,1},{6,2},{7,3},{8,12},{9,13},{10,... | collective-permute-start | bytes 6291464 | tf_op jit(solution)/shard_map/ppermute | solution.py:1072
  266.8 14.5 %local_rest_gradient.1 = (bf16[4,4,2,128,256]{4,3,2,1,0:T(8,128)(2,1)}, bf16[4,4,2,128,256]{4,3,2,1,0:T(8,128)(2,1)}) custom-call(s32[3]{0:T(128)} %pad_add_fusion.3.at_ref, bf16[768,7168]{1,0:T(8,128)(2,1)} %bitcast.170, bf16[768,7168]{1,0:T(8,128)(2,1)} %collective-permute-done.29.left_in.right_in.refs_1_.refs_3_.refs_5_, bf16[768,7168]{1,0:T(8,128)(2,1)} %bitcast.171, ...), custom_call_target="tpu_custom_call" | custom-call | flops 11000000 | bytes 10000 | tf_op jit(solution)/shard_map/local_rest_gradient/pallas_call | solution.py:876
  290.3 4.9 %frame_attention_back.1 = (bf16[1024,256]{1,0:T(8,128)(2,1)}, bf16[1024,256]{1,0:T(8,128)(2,1)}, bf16[1024,256]{1,0:T(8,128)(2,1)}) custom-call(s32[3]{0:T(128)} %pad_add_fusion.3.at_ref, bf16[1024,256]{1,0:T(8,128)(2,1)} %get-tuple-element.196.q_ref, bf16[1024,256]{1,0:T(8,128)(2,1)} %get-tuple-element.197.k_ref, ...), custom_call_target="tpu_custom_call" | custom-call | flops 11000000 | bytes 10000 | tf_op jit(solution)/shard_map/frame_attention_back/pallas_call | solution.py:612
  329.0 18.2 %collective-permute-done.43 = bf16[2,128,2048]{2,1,0:T(8,128)(2,1)S(1)} collective-permute-done((bf16[2,128,2048]{2,1,0:T(8,128)(2,1)S(1)}, bf16[2,128,2048]{2,1,0:T(8,128)(2,1)S(1)}, u32[]{:S(2)}, u32[]{:S(2)}) %collective-permute-start.43) | collective-permute-done | bytes 1048608 | tf_op jit(solution)/shard_map/ppermute | solution.py:1072
  349.6 18.9 %collective-permute-done.44 = bf16[2,128,2048]{2,1,0:T(8,128)(2,1)S(1)} collective-permute-done((bf16[2,128,2048]{2,1,0:T(8,128)(2,1)S(1)}, bf16[2,128,2048]{2,1,0:T(8,128)(2,1)S(1)}, u32[]{:S(2)}, u32[]{:S(2)}) %collective-permute-start.44) | collective-permute-done | bytes 1048608 | tf_op jit(solution)/shard_map/ppermute | solution.py:1072
  387.6 20.3 %collective-permute-done.53 = bf16[2,64,1024]{2,1,0:T(8,128)(2,1)S(1)} collective-permute-done((bf16[2,64,1024]{2,1,0:T(8,128)(2,1)S(1)}, bf16[2,64,1024]{2,1,0:T(8,128)(2,1)S(1)}, u32[]{:S(2)}, u32[]{:S(2)}) %collective-permute-start.53) | collective-permute-done | bytes 262176 | tf_op jit(solution)/shard_map/ppermute | solution.py:1072
  407.9 6.3 %collective-permute-done.50 = bf16[128,2048]{1,0:T(8,128)(2,1)S(1)} collective-permute-done((bf16[128,2048]{1,0:T(8,128)(2,1)S(1)}, bf16[128,2048]{1,0:T(8,128)(2,1)S(1)}, u32[]{:S(2)}, u32[]{:S(2)}) %collective-permute-start.50) | collective-permute-done | bytes 524320 | tf_op jit(solution)/shard_map/ppermute | solution.py:1072
  426.0 5.3 %collective-permute-done.54 = bf16[2,64,1024]{2,1,0:T(8,128)(2,1)S(1)} collective-permute-done((bf16[2,64,1024]{2,1,0:T(8,128)(2,1)S(1)}, bf16[2,64,1024]{2,1,0:T(8,128)(2,1)S(1)}, u32[]{:S(2)}, u32[]{:S(2)}) %collective-permute-start.54) | collective-permute-done | bytes 262176 | tf_op jit(solution)/shard_map/ppermute | solution.py:1072
  431.3 16.0 %collective-permute-done.56 = bf16[2,208,512]{2,1,0:T(8,128)(2,1)S(1)} collective-permute-done((bf16[2,208,512]{2,1,0:T(8,128)(2,1)S(1)}, bf16[2,208,512]{2,1,0:T(8,128)(2,1)S(1)}, u32[]{:S(2)}, u32[]{:S(2)}) %collective-permute-start.56) | collective-permute-done | bytes 426016 | tf_op jit(solution)/shard_map/ppermute | solution.py:1072
  453.3 8.6 %collective-permute-done.60 = bf16[208,512]{1,0:T(8,128)(2,1)} collective-permute-done((bf16[208,512]{1,0:T(8,128)(2,1)}, bf16[208,512]{1,0:T(8,128)(2,1)}, u32[]{:S(2)}, u32[]{:S(2)}) %collective-permute-start.60) | collective-permute-done | bytes 213024 | tf_op jit(solution)/shard_map/ppermute | solution.py:1072
  (353 shorter events, 175.8 us)
Async XLA Ops:
  5.9 29.9 %collective-permute-start.8 = (bf16[1,3,64,1024]{3,2,1,0:T(8,128)(2,1)S(1)}, bf16[1,3,64,1024]{3,2,1,0:T(8,128)(2,1)S(1)}, u32[]{:S(2)}, u32[]{:S(2)}) collective-permute-start(bf16[1,3,64,1024]{3,2,1,0:T(8,128)(2,1)S(1)} %get-tuple-element.301), channel_id=1, source_target_pairs={{16,28},{17,29},{18,30},{19,31},{20,24},{21,25},{22,26},{23,27},{2... | collective-permute-start | bytes 1179656 | tf_op jit(solution)/shard_map/ppermute | solution.py:1072
  61.5 42.7 %collective-permute-start.20 = (bf16[3,1024,512]{2,1,0:T(8,128)(2,1)}, bf16[3,1024,512]{2,1,0:T(8,128)(2,1)}, u32[]{:S(2)}, u32[]{:S(2)}) collective-permute-start(bf16[3,1024,512]{2,1,0:T(8,128)(2,1)} %bitcast.201), channel_id=1, source_target_pairs={{0,1},{1,0},{2,3},{3,2},{4,5},{5,4},{6,7},{7,6},{8,9},{9,8},{10,11... | collective-permute-start | bytes 9437192 | tf_op jit(solution)/shard_map/ppermute | solution.py:1072
  68.7 28.4 %collective-permute-start.13 = (s32[3,256]{1,0:T(4,128)S(1)}, s32[3,256]{1,0:T(4,128)S(1)}, u32[]{:S(2)}, u32[]{:S(2)}) collective-permute-start(s32[3,256]{1,0:T(4,128)S(1)} %reshape.396), channel_id=1, source_target_pairs={{0,1},{1,0},{2,3},{3,2},{4,5},{5,4},{6,7},{7,6},{8,9},{9,8},{10,11... | collective-permute-start | bytes 9224 | tf_op jit(solution)/shard_map/ppermute | solution.py:1072
  68.7 31.4 %collective-permute-start.14 = (bf16[768,1024]{1,0:T(8,128)(2,1)}, bf16[768,1024]{1,0:T(8,128)(2,1)S(1)}, u32[]{:S(2)}, u32[]{:S(2)}) collective-permute-start(bf16[768,1024]{1,0:T(8,128)(2,1)} %bitcast.20.cot_ref.left), channel_id=1, source_target_pairs={{0,1},{1,0},{2,3},{3,2},{4,5},{5,4},{6,7},{7,6},{8,9},{9,8},{10,11... | collective-permute-start | bytes 4718600 | tf_op jit(solution)/shard_map/ppermute | solution.py:1072
  76.9 28.0 %collective-permute-start.19 = (bf16[256,1024]{1,0:T(8,128)(2,1)}, bf16[256,1024]{1,0:T(8,128)(2,1)}, u32[]{:S(2)}, u32[]{:S(2)}) collective-permute-start(bf16[256,1024]{1,0:T(8,128)(2,1)} %get-tuple-element.148), channel_id=1, source_target_pairs={{0,16},{1,17},{2,18},{3,19},{4,20},{5,21},{6,22},{7,23},{8,24},{9,... | collective-permute-start | bytes 1572872 | tf_op jit(solution)/shard_map/ppermute | solution.py:1084
  102.9 56.7 %collective-permute-start.24 = (bf16[4,64,1024]{2,1,0:T(8,128)(2,1)}, bf16[4,64,1024]{2,1,0:T(8,128)(2,1)}, u32[]{:S(2)}, u32[]{:S(2)}) collective-permute-start(bf16[4,64,1024]{2,1,0:T(8,128)(2,1)} %constant_dynamic-update-slice_fusion.8), channel_id=1, source_target_pairs={{0,16},{1,17},{2,18},{3,19},{4,20},{5,21},{6,22},{7,23},{8,24},{9,... | collective-permute-start | bytes 1572872 | tf_op jit(solution)/shard_map/ppermute | solution.py:1084
  191.1 65.3 %collective-permute-start.30 = (bf16[256,1024]{1,0:T(8,128)(2,1)}, bf16[256,1024]{1,0:T(8,128)(2,1)}, u32[]{:S(2)}, u32[]{:S(2)}) collective-permute-start(bf16[256,1024]{1,0:T(8,128)(2,1)} %get-tuple-element.175.left), channel_id=1, source_target_pairs={{0,1},{1,0},{2,3},{3,2},{4,5},{5,4},{6,7},{7,6},{8,9},{9,8},{10,11... | collective-permute-start | bytes 1572872 | tf_op jit(solution)/shard_map/ppermute | solution.py:1072
  191.2 30.1 %collective-permute-start.31 = (bf16[256,2048]{1,0:T(8,128)(2,1)S(1)}, bf16[256,2048]{1,0:T(8,128)(2,1)}, u32[]{:S(2)}, u32[]{:S(2)}) collective-permute-start(bf16[256,2048]{1,0:T(8,128)(2,1)S(1)} %copy-done.42), channel_id=1, source_target_pairs={{0,1},{1,0},{2,3},{3,2},{4,5},{5,4},{6,7},{7,6},{8,9},{9,8},{10,11... | collective-permute-start | bytes 3145736 | tf_op jit(solution)/shard_map/ppermute | solution.py:1072
  211.9 36.5 %collective-permute-start.35 = (bf16[256,2048]{1,0:T(8,128)(2,1)}, bf16[256,2048]{1,0:T(8,128)(2,1)}, u32[]{:S(2)}, u32[]{:S(2)}) collective-permute-start(bf16[256,2048]{1,0:T(8,128)(2,1)} %get-tuple-element.185), channel_id=1, source_target_pairs={{0,1},{1,0},{2,3},{3,2},{4,5},{5,4},{6,7},{7,6},{8,9},{9,8},{10,11... | collective-permute-start | bytes 3145736 | tf_op jit(solution)/shard_map/ppermute | solution.py:1072
  216.7 30.2 %collective-permute-start.33 = (bf16[1,3,64,1024]{3,2,1,0:T(8,128)(2,1)S(1)}, bf16[1,3,64,1024]{3,2,1,0:T(8,128)(2,1)S(1)}, u32[]{:S(2)}, u32[]{:S(2)}) collective-permute-start(bf16[1,3,64,1024]{3,2,1,0:T(8,128)(2,1)S(1)} %get-tuple-element.304), channel_id=1, source_target_pairs={{16,24},{17,25},{18,26},{19,27},{20,28},{21,29},{22,30},{23,31},{2... | collective-permute-start | bytes 1179656 | tf_op jit(solution)/shard_map/ppermute | solution.py:1072
  248.4 56.1 %collective-permute-start.39 = (bf16[2,2,128,2048]{3,2,1,0:T(8,128)(2,1)S(1)}, bf16[2,2,128,2048]{3,2,1,0:T(8,128)(2,1)}, u32[]{:S(2)}, u32[]{:S(2)}) collective-permute-start(bf16[2,2,128,2048]{3,2,1,0:T(8,128)(2,1)S(1)} %broadcast_select_fusion), channel_id=1, source_target_pairs={{0,4},{1,5},{2,6},{3,7},{4,0},{5,1},{6,2},{7,3},{8,12},{9,13},{10,... | collective-permute-start | bytes 6291464 | tf_op jit(solution)/shard_map/ppermute | solution.py:1072
  262.6 45.7 %collective-permute-start.40 = (bf16[4,128,2048]{2,1,0:T(8,128)(2,1)}, bf16[4,128,2048]{2,1,0:T(8,128)(2,1)}, u32[]{:S(2)}, u32[]{:S(2)}) collective-permute-start(bf16[4,128,2048]{2,1,0:T(8,128)(2,1)} %broadcast_select_fusion.1), channel_id=1, source_target_pairs={{0,2},{1,3},{2,0},{3,1},{4,6},{5,7},{6,4},{7,5},{8,10},{9,11},{10,... | collective-permute-start | bytes 6291464 | tf_op jit(solution)/shard_map/ppermute | solution.py:1072
  284.0 43.1 %collective-permute-start.46 = (bf16[2,4,3,64,512]{4,3,2,1,0:T(8,128)(2,1)}, bf16[2,4,3,64,512]{4,3,2,1,0:T(8,128)(2,1)}, u32[]{:S(2)}, u32[]{:S(2)}) collective-permute-start(bf16[2,4,3,64,512]{4,3,2,1,0:T(8,128)(2,1)} %get-tuple-element.220), channel_id=1, source_target_pairs={{16,0},{17,1},{18,2},{19,3},{20,4},{21,5},{22,6},{23,7},{24,8},{25... | collective-permute-start | bytes 4718600 | tf_op jit(solution)/shard_map/ppermute | solution.py:1087
  308.3 60.2 %collective-permute-start.42 = (bf16[4,4,2,128,256]{4,3,2,1,0:T(8,128)(2,1)S(1)}, bf16[4,4,2,128,256]{4,3,2,1,0:T(8,128)(2,1)S(1)}, u32[]{:S(2)}, u32[]{:S(2)}) collective-permute-start(bf16[4,4,2,128,256]{4,3,2,1,0:T(8,128)(2,1)S(1)} %maximum_select_fusion.1), channel_id=1, source_target_pairs={{0,2},{1,3},{2,0},{3,1},{4,6},{5,7},{6,4},{7,5},{8,10},{9,11},{10,... | collective-permute-start | bytes 6291464 | tf_op jit(solution)/shard_map/ppermute | solution.py:1072
  312.4 34.8 %collective-permute-start.43 = (bf16[2,128,2048]{2,1,0:T(8,128)(2,1)S(1)}, bf16[2,128,2048]{2,1,0:T(8,128)(2,1)S(1)}, u32[]{:S(2)}, u32[]{:S(2)}) collective-permute-start(bf16[2,128,2048]{2,1,0:T(8,128)(2,1)S(1)} %slice.235), channel_id=1, source_target_pairs={{0,4},{1,5},{2,6},{3,7},{4,0},{5,1},{6,2},{7,3},{8,12},{9,13},{10,... | collective-permute-start | bytes 3145736 | tf_op jit(solution)/shard_map/ppermute | solution.py:1072
  321.9 46.7 %collective-permute-start.44 = (bf16[2,128,2048]{2,1,0:T(8,128)(2,1)S(1)}, bf16[2,128,2048]{2,1,0:T(8,128)(2,1)S(1)}, u32[]{:S(2)}, u32[]{:S(2)}) collective-permute-start(bf16[2,128,2048]{2,1,0:T(8,128)(2,1)S(1)} %slice_bitcast_fusion.1), channel_id=1, source_target_pairs={{0,8},{1,9},{2,10},{3,11},{4,12},{5,13},{6,14},{7,15},{8,0},{9,1},... | collective-permute-start | bytes 3145736 | tf_op jit(solution)/shard_map/ppermute | solution.py:1072
  325.3 43.3 %collective-permute-start.45 = (bf16[256,1024]{1,0:T(8,128)(2,1)S(1)}, bf16[256,1024]{1,0:T(8,128)(2,1)S(1)}, u32[]{:S(2)}, u32[]{:S(2)}) collective-permute-start(bf16[256,1024]{1,0:T(8,128)(2,1)S(1)} %slice.314), channel_id=1, source_target_pairs={{0,2},{1,3},{2,0},{3,1},{4,6},{5,7},{6,4},{7,5},{8,10},{9,11},{10,... | collective-permute-start | bytes 1572872 | tf_op jit(solution)/shard_map/ppermute | solution.py:1072
  327.2 55.8 %collective-permute-start.58 = (bf16[4,64,1024]{2,1,0:T(8,128)(2,1)S(1)}, bf16[4,64,1024]{2,1,0:T(8,128)(2,1)}, u32[]{:S(2)}, u32[]{:S(2)}) collective-permute-start(bf16[4,64,1024]{2,1,0:T(8,128)(2,1)S(1)} %broadcast_select_fusion.8), channel_id=1, source_target_pairs={{0,1},{1,0},{2,3},{3,2},{4,5},{5,4},{6,7},{7,6},{8,9},{9,8},{10,11... | collective-permute-start | bytes 1572872 | tf_op jit(solution)/shard_map/ppermute | solution.py:1072
  347.2 37.5 %collective-permute-start.52 = (bf16[4,3,64,1024]{3,2,1,0:T(8,128)(2,1)}, bf16[4,3,64,1024]{3,2,1,0:T(8,128)(2,1)}, u32[]{:S(2)}, u32[]{:S(2)}) collective-permute-start(bf16[4,3,64,1024]{3,2,1,0:T(8,128)(2,1)} %constant_dynamic-update-slice_fusion.5), channel_id=1, source_target_pairs={{16,0},{17,1},{18,2},{19,3},{20,4},{21,5},{22,6},{23,7},{24,8},{25... | collective-permute-start | bytes 4718600 | tf_op jit(solution)/shard_map/ppermute | solution.py:1087
  370.5 43.8 %collective-permute-start.48 = (bf16[2,4,2,128,256]{4,3,2,1,0:T(8,128)(2,1)}, bf16[2,4,2,128,256]{4,3,2,1,0:T(8,128)(2,1)}, u32[]{:S(2)}, u32[]{:S(2)}) collective-permute-start(bf16[2,4,2,128,256]{4,3,2,1,0:T(8,128)(2,1)} %slice.202), channel_id=1, source_target_pairs={{0,4},{1,5},{2,6},{3,7},{4,0},{5,1},{6,2},{7,3},{8,12},{9,13},{10,... | collective-permute-start | bytes 3145736 | tf_op jit(solution)/shard_map/ppermute | solution.py:1072
  371.9 36.0 %collective-permute-start.49 = (bf16[128,2048]{1,0:T(8,128)(2,1)}, bf16[128,2048]{1,0:T(8,128)(2,1)}, u32[]{:S(2)}, u32[]{:S(2)}) collective-permute-start(bf16[128,2048]{1,0:T(8,128)(2,1)} %slice_bitcast_fusion.8), channel_id=1, source_target_pairs={{0,8},{1,9},{2,10},{3,11},{4,12},{5,13},{6,14},{7,15},{8,0},{9,1},... | collective-permute-start | bytes 1572872 | tf_op jit(solution)/shard_map/ppermute | solution.py:1072
  382.6 31.7 %collective-permute-start.51 = (bf16[4,208,512]{2,1,0:T(8,128)(2,1)S(1)}, bf16[4,208,512]{2,1,0:T(8,128)(2,1)S(1)}, u32[]{:S(2)}, u32[]{:S(2)}) collective-permute-start(bf16[4,208,512]{2,1,0:T(8,128)(2,1)S(1)} %slice_bitcast_fusion.2), channel_id=1, source_target_pairs={{0,2},{1,3},{2,0},{3,1},{4,6},{5,7},{6,4},{7,5},{8,10},{9,11},{10,... | collective-permute-start | bytes 2555912 | tf_op jit(solution)/shard_map/ppermute | solution.py:1072
  382.9 31.4 %collective-permute-start.50 = (bf16[128,2048]{1,0:T(8,128)(2,1)S(1)}, bf16[128,2048]{1,0:T(8,128)(2,1)S(1)}, u32[]{:S(2)}, u32[]{:S(2)}) collective-permute-start(bf16[128,2048]{1,0:T(8,128)(2,1)S(1)} %copy-done.32), channel_id=1, source_target_pairs={{0,2},{1,3},{2,0},{3,1},{4,6},{5,7},{6,4},{7,5},{8,10},{9,11},{10,... | collective-permute-start | bytes 1572872 | tf_op jit(solution)/shard_map/ppermute | solution.py:1072
  419.0 28.2 %collective-permute-start.55 = (bf16[4,2,128,256]{3,2,1,0:T(8,128)(2,1)S(1)}, bf16[4,2,128,256]{3,2,1,0:T(8,128)(2,1)S(1)}, u32[]{:S(2)}, u32[]{:S(2)}) collective-permute-start(bf16[4,2,128,256]{3,2,1,0:T(8,128)(2,1)S(1)} %slice_bitcast_fusion.17), channel_id=1, source_target_pairs={{0,8},{1,9},{2,10},{3,11},{4,12},{5,13},{6,14},{7,15},{8,0},{9,1},... | collective-permute-start | bytes 1572872 | tf_op jit(solution)/shard_map/ppermute | solution.py:1072
  (88 other events, 806.1 us)

commit v2 on v1

--- a/solution.py
+++ b/solution.py
@@ -781,7 +781,15 @@
                 (theirs_ref if jy else mine_ref)[low * 2 + high] = part
 
 
-def weight_kernel(at_ref, left, left_in, right, right_in, mine_ref, theirs_ref, total_ref, turned, turned_in, *, here, plane_first):
+def weight_kernel(at_ref, left, left_in, right, right_in, *refs, here, plane_first):
+    other, (mine_ref, theirs_ref, total_ref, turned, turned_in) = refs[:-5], refs[-5:]
+
+    if other:
+
+        @pl.when(at_ref[0] != here)
+        def _():
+            theirs_ref[...] = other[0][...]
+
     @pl.when(at_ref[0] == here)
     def _():
         @pl.when(pl.program_id(0) == 0)
@@ -793,7 +801,7 @@
         deal(total_ref, at_ref, mine_ref, theirs_ref, plane_first)
 
 
-def weight_call(at, here, four, skip, plane_first, name, us, width, cols, chunk=512):
+def weight_call(at, here, four, skip, plane_first, name, us, width, cols, other=None, chunk=512):
     piece = width // 8
     now = lambda i, s: jnp.where(s[0] == here, i, 0)
     whole = [
@@ -805,24 +813,27 @@
     ]
     if plane_first:
         shape = jax.ShapeDtypeStruct((2, 2, piece, cols), bf)
-        out = pl.BlockSpec((2, 2, piece, chunk), lambda i, s: (0, 0, 0, now(i, s)))
     else:
         shape = jax.ShapeDtypeStruct((4, piece, cols), bf)
-        out = pl.BlockSpec((4, piece, chunk), lambda i, s: (0, 0, now(i, s)))
+    block = lambda at_col: pl.BlockSpec(
+        shape.shape[:-1] + (chunk,), lambda i, s: (0,) * (len(shape.shape) - 1) + (at_col(i, s),)
+    )
+    passed = () if other is None else (other,)
+    theirs = block(now) if other is None else block(lambda i, s: i)
     return pl.pallas_call(
         functools.partial(weight_kernel, here=here, plane_first=plane_first),
         grid_spec=pltpu.PrefetchScalarGridSpec(
             num_scalar_prefetch=1,
             grid=(cols // chunk,),
-            in_specs=whole + part,
-            out_specs=(out, out),
+            in_specs=whole + part + [block(lambda i, s: jnp.where(s[0] == here, 0, i)) for _ in passed],
+            out_specs=(block(now), theirs),
             scratch_shapes=[pltpu.VMEM((width, chunk), f32)] + [pltpu.VMEM((width, a.shape[0]), bf) for a in four[:2]],
         ),
         out_shape=(shape, shape),
         compiler_params=pltpu.CompilerParams(vmem_limit_bytes=60 * 1024 * 1024),
         cost_estimate=lasting(us),
         name=name,
-    )(at, *four)
+    )(at, *four, *passed)
 
 
 def rest_kernel(at_ref, *refs, here):
@@ -1200,22 +1211,20 @@
     local_moved = planes_out(local_low, second)
     low_side = side_swap(low_own, first)
     down_mine, down_theirs = weight_call(
-        at, 0, (grad_low, grad_in_low, act_own, act_in), (0, 0, 0, 0), True, "down_gradient", 8, width, hidden
+        at, 0, (grad_low, grad_in_low, act_own, act_in), (0, 0, 0, 0), True, "down_gradient", 8, width, hidden, l_down_theirs
     )
     l_up_mine, l_up_theirs = weight_call(
         at, 1, (flat(l_send), l_got, flat(l_rise), l_got),
         (hidden // width, hidden // width, 0, 0), False, "local_up_gradient", 4, width, hidden,
     )
-    down_theirs = jnp.where(on_first, down_theirs, l_down_theirs)
     (down_theirs, l_up_theirs, local_moved), (rise_in, table_low) = fence(
         (down_theirs, l_up_theirs, local_moved), (rise_in, table_low)
     )
     table_moved = to_global(table_low)
     down_got = swap(down_theirs, 1)
     up_mine, up_theirs = weight_call(
-        at, 0, (mid, mid_in, rise_own, rise_in), (0, 0, 0, 0), False, "up_gradient", 8, width, hidden
-    )
-    up_theirs = jnp.where(on_first, up_theirs, l_up_theirs)
+        at, 0, (mid, mid_in, rise_own, rise_in), (0, 0, 0, 0), False, "up_gradient", 8, width, hidden, l_up_theirs
+    )
     (up_theirs, low_side), (l_pack, l_act) = fence((up_theirs, low_side), (l_pack, l_act))
     up_got = swap(up_theirs, 0)
     low_at = hidden // width + 1

time: 476 us -> 473 us (level)
  other arithmetic: 44.6 us -> 38.2 us
  Pallas kernels: 166 us -> 171 us
    select_n x2 -> x0, other arithmetic: 4.99 us -> none  [the longest x1 3.18 us: body(): up_theirs = jnp.where(on_first, up_theirs, l_up_theirs)]
  transfers between devices with their start and end apart: 62 -> 62, of which waited for: 12 -> 12; matrix products, arithmetic and copies ran while one was open for 17% -> 16% of each run, Pallas kernels for 36% -> 37%
where the time goes in v2:
time: 473 us; the launch traced here: 465 us
  Pallas kernels  171 us (36%)
  waiting for transfers between devices  113 us (24%)
  starting transfers between devices  94.2 us (20%)
  local copies, waits for them, and re-layouts  43 us (9%)
  other arithmetic  38.2 us (8%)
    ppermute x57, waiting for transfers between devices, linked(): return lax.ppermute(a, ('section', 'dp', 'tensor'), pairs)  113 us
    ppermute x57, starting transfers between devices, linked(): return lax.ppermute(a, ('section', 'dp', 'tensor'), pairs)  85.4 us
    pallas_call x1, Pallas kernels, local_call(): pl.pallas_call(local_skip, grid_spec=pltpu.PrefetchScalarGridSpec(num_sca...  54.6 us
    pallas_call x4, Pallas kernels, weight_call(): pl.pallas_call(functools.partial(weight_kernel, here=here, plane_first=pl...  36.5 us
    pallas_call x2, Pallas kernels, rest_call(): pl.pallas_call(functools.partial(rest_kernel, here=here), grid_spec=pltpu...  18.6 us
    pallas_call x1, Pallas kernels, prepare_call(): pl.pallas_call(prepare_kernel, grid_spec=pltpu.PrefetchScalarGridSpec(num...  17.1 us
    pallas_call x1, Pallas kernels, fall_call(): pl.pallas_call(fall_kernel, grid_spec=pltpu.PrefetchScalarGridSpec(num_sc...  13.9 us
    unnamed x108, local copies, waits for them, and re-layouts  11.8 us
  transfers between devices with their start and end apart: 62, of which 12 were waited for; matrix products, arithmetic and copies ran while one was open for 16% of the time, Pallas kernels for 37%

profile of v2, /device:TPU:3, one launch (start us, length us, event | category | flops | bytes accessed | tf_op | source)
XLA Modules:
  0.0 465.5 jit_solution(7210727568331782266)
XLA Ops:
  5.9 5.2 %collective-permute-start.8 = (bf16[1,3,64,1024]{3,2,1,0:T(8,128)(2,1)S(1)}, bf16[1,3,64,1024]{3,2,1,0:T(8,128)(2,1)S(1)}, u32[]{:S(2)}, u32[]{:S(2)}) collective-permute-start(bf16[1,3,64,1024]{3,2,1,0:T(8,128)(2,1)S(1)} %get-tuple-element.301), channel_id=1, source_target_pairs={{16,28},{17,29},{18,30},{19,31},{20,24},{21,25},{22,26},{23,27},{2... | collective-permute-start | bytes 1179656 | tf_op jit(solution)/shard_map/ppermute | solution.py:1083
  16.4 5.0 %collective-permute-start.9 = (s32[1,3,64]{2,0,1:T(1,128)S(1)}, s32[1,3,64]{2,0,1:T(1,128)S(1)}, u32[]{:S(2)}, u32[]{:S(2)}) collective-permute-start(s32[1,3,64]{2,0,1:T(1,128)S(1)} %get-tuple-element.325), channel_id=1, source_target_pairs={{16,20},{17,21},{18,22},{19,23},{20,16},{21,17},{22,18},{23,19},{2... | collective-permute-start | bytes 2312 | tf_op jit(solution)/shard_map/ppermute | solution.py:1083
  24.1 6.3 %collective-permute-start.7 = (bf16[1,3,64,1024]{3,2,1,0:T(8,128)(2,1)S(1)}, bf16[1,3,64,1024]{3,2,1,0:T(8,128)(2,1)S(1)}, u32[]{:S(2)}, u32[]{:S(2)}) collective-permute-start(bf16[1,3,64,1024]{3,2,1,0:T(8,128)(2,1)S(1)} %get-tuple-element.302), channel_id=1, source_target_pairs={{16,24},{17,25},{18,26},{19,27},{20,28},{21,29},{22,30},{23,31},{2... | collective-permute-start | bytes 1179656 | tf_op jit(solution)/shard_map/ppermute | solution.py:1083
  35.8 11.2 %collective-permute-done.7 = bf16[1,3,64,1024]{3,2,1,0:T(8,128)(2,1)S(1)} collective-permute-done((bf16[1,3,64,1024]{3,2,1,0:T(8,128)(2,1)S(1)}, bf16[1,3,64,1024]{3,2,1,0:T(8,128)(2,1)S(1)}, u32[]{:S(2)}, u32[]{:S(2)}) %collective-permute-start.7) | collective-permute-done | bytes 393248 | tf_op jit(solution)/shard_map/ppermute | solution.py:1083
  54.8 5.8 %frame_attention.1 = (bf16[1024,1024]{1,0:T(8,128)(2,1)}, bf16[1024,256]{1,0:T(8,128)(2,1)}, bf16[1024,256]{1,0:T(8,128)(2,1)}, bf16[1024,256]{1,0:T(8,128)(2,1)...) custom-call(s32[3]{0:T(128)} %pad_add_fusion.3.at_ref, bf16[256,1024]{1,0:T(8,128)(2,1)} %bitcast.176, ...), custom_call_target="tpu_custom_call" | custom-call | flops 19800000512 | bytes 18000000 | tf_op jit(solution)/shard_map/frame_attention/pallas_call | solution.py:540
  69.7 7.2 %global_forward.1 = (f32[256,1024]{1,0:T(8,128)}, bf16[256,1024]{1,0:T(8,128)(2,1)}, bf16[256,2048]{1,0:T(8,128)(2,1)}, bf16[256,2048]{1,0:T(8,128)(2,1)}, bf16[...) custom-call(s32[3]{0:T(128)} %pad_add_fusion.3.at_ref, bf16[256,1024]{1,0:T(8,128)(2,1)} %bitcast.177, ...), custom_call_target="tpu_custom_call" | custom-call | flops 16499999744 | bytes 15000000 | tf_op jit(solution)/shard_map/global_forward/pallas_call | solution.py:685
  80.0 17.1 %local_prepare.1 = (bf16[3,256,1024]{2,1,0:T(8,128)(2,1)}, bf16[3,256,2048]{2,1,0:T(8,128)(2,1)}, bf16[3,256,2048]{2,1,0:T(8,128)(2,1)}) custom-call(s32[3]{0:T(128)} %pad_add_fusion.3.at_ref, s32[3,256,1]{2,1,0:T(8,128)} %broadcast_in_dim_reshape.8.code_ref, bf16[768,1024]{1,0:T(8,128)(2,1)} %bitcast.20.cot_ref.left, bf16[2048,1024]{1,0:T(8,128)(2,1)} %bitcast.181, ...), custom_call_target="tpu_custom_call" | custom-call | flops 5500000256 | bytes 5000000 | tf_op jit(solution)/shard_map/local_prepare/pallas_call | solution.py:1028
  104.9 54.6 %local_layer.1 = (f32[3,256,1024]{2,1,0:T(8,128)}, bf16[3,256,2048]{2,1,0:T(8,128)(2,1)}, bf16[3,256,2048]{2,1,0:T(8,128)(2,1)}, bf16[4,3,256,512]{3,2,1,0:T(8,1...) custom-call(s32[3]{0:T(128)} %pad_add_fusion.3.at_ref, ...), custom_call_target="tpu_custom_call" | custom-call | flops 62699999232 | bytes 57000000 | tf_op jit(solution)/shard_map/local_layer/pallas_call | solution.py:477
  169.9 5.8 %table_gradient.1 = (bf16[2,4,3,64,512]{4,3,2,1,0:T(8,128)(2,1)}, bf16[2,4,3,64,512]{4,3,2,1,0:T(8,128)(2,1)}) custom-call(s32[3]{0:T(128)} %pad_add_fusion.3.at_ref, s32[3,1,256]{2,1,0:T(1,128)} %broadcast_in_dim_reshape.6.code_ref, s32[3,1,256]{2,1,0:T(1,128)} %broadcast_in_dim.21.code_in_ref, bf16[3,256,512]{2,1,0:T(8,128)(2,1)} %get-tuple-element.308.own_ref, ...), custom_call_target="tpu_custom_call" | custom-call | flops 4400000000 | bytes 4000000 | tf_op jit(solution)/shard_map/table_gradient/pallas_call | solution.py:980
  175.8 12.8 %local_down_gradient.1 = (bf16[2,2,128,2048]{3,2,1,0:T(8,128)(2,1)}, bf16[2,2,128,2048]{3,2,1,0:T(8,128)(2,1)}) custom-call(s32[3]{0:T(128)} %pad_add_fusion.3.at_ref, bf16[768,1024]{1,0:T(8,128)(2,1)} %bitcast.20.cot_ref.left, bf16[768,1024]{1,0:T(8,128)(2,1)} %copy-done.40, bf16[768,2048]{1,0:T(8,128)(2,1)} %bitcast.188, ...), custom_call_target="tpu_custom_call" | custom-call | flops 4400000000 | bytes 4000000 | tf_op jit(solution)/shard_map/local_down_gradient/pallas_call | solution.py:823
  191.5 13.9 %local_output.1 = bf16[4,3,64,1024]{3,2,1,0:T(8,128)(2,1)} custom-call(s32[3]{0:T(128)} %pad_add_fusion.3.at_ref, f32[768,1024]{1,0:T(8,128)} %bitcast.187, bf16[768,2048]{1,0:T(8,128)(2,1)} %bitcast.189, bf16[768,2048]{1,0:T(8,128)(2,1)} %bitcast.191, bf16[2048,1024]{1,0:T(8,128)(2,1)} %bitcast.182, bf16[2048,1024]{1,0:T(8,128)(2,1)} %collective-permute-done.12.dx_ref), custom_call_target="tpu_custom_call" | custom-call | flops 11000000 | bytes 10000 | tf_op jit(solution)/shard_map/local_output/pallas_call | solution.py:938
  205.5 6.4 %global_backward.1 = (bf16[256,2048]{1,0:T(8,128)(2,1)}, bf16[256,2048]{1,0:T(8,128)(2,1)}, f32[256,1024]{1,0:T(8,128)}, bf16[256,1024]{1,0:T(8,128)(2,1)}, f32[1,1024]{1,0:T(1,128)}) custom-call(s32[3]{0:T(128)} %pad_add_fusion.3.at_ref, bf16[256,1024]{1,0:T(8,128)(2,1)} %copy-done.45, f32[256,1024]{1,0:T(8,128)} %get-tuple-element.166.resid_ref, ...), custom_call_target="tpu_custom_call" | custom-call | flops 14300000256 | bytes 13000000 | tf_op jit(solution)/shard_map/global_backward/pallas_call | solution.py:747
  223.9 5.7 %down_gradient.1 = (bf16[2,2,128,2048]{3,2,1,0:T(8,128)(2,1)}, bf16[2,2,128,2048]{3,2,1,0:T(8,128)(2,1)}) custom-call(s32[3]{0:T(128)} %pad_add_fusion.3.at_ref, bf16[256,1024]{1,0:T(8,128)(2,1)} %copy-done.45, bf16[256,1024]{1,0:T(8,128)(2,1)} %copy-done.48, bf16[256,2048]{1,0:T(8,128)(2,1)} %get-tuple-element.178.right, ...), custom_call_target="tpu_custom_call" | custom-call | flops 8800000000 | bytes 8000000 | tf_op jit(solution)/shard_map/down_gradient/pallas_call | solution.py:823
  229.6 12.7 %local_up_gradient.1 = (bf16[4,128,2048]{2,1,0:T(8,128)(2,1)}, bf16[4,128,2048]{2,1,0:T(8,128)(2,1)}) custom-call(s32[3]{0:T(128)} %pad_add_fusion.3.at_ref, bf16[768,7168]{1,0:T(8,128)(2,1)} %bitcast.169, bf16[768,7168]{1,0:T(8,128)(2,1)} %collective-permute-done.29.left_in.right_in.refs_1_.refs_3_.refs_5_, bf16[768,2048]{1,0:T(8,128)(2,1)} %bitcast.185, ...), custom_call_target="tpu_custom_call" | custom-call | flops 4400000000 | bytes 4000000 | tf_op jit(solution)/shard_map/local_up_gradient/pallas_call | solution.py:823
  248.3 7.9 %collective-permute-start.39 = (bf16[2,2,128,2048]{3,2,1,0:T(8,128)(2,1)}, bf16[2,2,128,2048]{3,2,1,0:T(8,128)(2,1)S(1)}, u32[]{:S(2)}, u32[]{:S(2)}) collective-permute-start(bf16[2,2,128,2048]{3,2,1,0:T(8,128)(2,1)} %get-tuple-element.204), channel_id=1, source_target_pairs={{0,4},{1,5},{2,6},{3,7},{4,0},{5,1},{6,2},{7,3},{8,12},{9,13},{10,... | collective-permute-start | bytes 6291464 | tf_op jit(solution)/shard_map/ppermute | solution.py:1083
  256.3 5.4 %up_gradient.1 = (bf16[4,128,2048]{2,1,0:T(8,128)(2,1)}, bf16[4,128,2048]{2,1,0:T(8,128)(2,1)}) custom-call(s32[3]{0:T(128)} %pad_add_fusion.3.at_ref, bf16[256,1024]{1,0:T(8,128)(2,1)} %get-tuple-element.175.left, bf16[256,1024]{1,0:T(8,128)(2,1)} %collective-permute-done.30.left_in, bf16[256,2048]{1,0:T(8,128)(2,1)} %get-tuple-element.176.right, ...), custom_call_target="tpu_custom_call" | custom-call | flops 8800000000 | bytes 8000000 | tf_op jit(solution)/shard_map/up_gradient/pallas_call | solution.py:823
  265.8 14.5 %local_rest_gradient.1 = (bf16[4,4,2,128,256]{4,3,2,1,0:T(8,128)(2,1)}, bf16[4,4,2,128,256]{4,3,2,1,0:T(8,128)(2,1)}) custom-call(s32[3]{0:T(128)} %pad_add_fusion.3.at_ref, bf16[768,7168]{1,0:T(8,128)(2,1)} %bitcast.170, bf16[768,7168]{1,0:T(8,128)(2,1)} %collective-permute-done.29.left_in.right_in.refs_1_.refs_3_.refs_5_, bf16[768,7168]{1,0:T(8,128)(2,1)} %bitcast.171, ...), custom_call_target="tpu_custom_call" | custom-call | flops 11000000 | bytes 10000 | tf_op jit(solution)/shard_map/local_rest_gradient/pallas_call | solution.py:887
  326.8 21.1 %collective-permute-done.43 = bf16[2,128,2048]{2,1,0:T(8,128)(2,1)S(1)} collective-permute-done((bf16[2,128,2048]{2,1,0:T(8,128)(2,1)S(1)}, bf16[2,128,2048]{2,1,0:T(8,128)(2,1)S(1)}, u32[]{:S(2)}, u32[]{:S(2)}) %collective-permute-start.43) | collective-permute-done | bytes 1048608 | tf_op jit(solution)/shard_map/ppermute | solution.py:1083
  350.4 15.9 %collective-permute-done.44 = bf16[2,128,2048]{2,1,0:T(8,128)(2,1)S(1)} collective-permute-done((bf16[2,128,2048]{2,1,0:T(8,128)(2,1)S(1)}, bf16[2,128,2048]{2,1,0:T(8,128)(2,1)S(1)}, u32[]{:S(2)}, u32[]{:S(2)}) %collective-permute-start.44) | collective-permute-done | bytes 1048608 | tf_op jit(solution)/shard_map/ppermute | solution.py:1083
  385.3 20.3 %collective-permute-done.53 = bf16[2,64,1024]{2,1,0:T(8,128)(2,1)S(1)} collective-permute-done((bf16[2,64,1024]{2,1,0:T(8,128)(2,1)S(1)}, bf16[2,64,1024]{2,1,0:T(8,128)(2,1)S(1)}, u32[]{:S(2)}, u32[]{:S(2)}) %collective-permute-start.53) | collective-permute-done | bytes 262176 | tf_op jit(solution)/shard_map/ppermute | solution.py:1083
  405.6 6.3 %collective-permute-done.50 = bf16[128,2048]{1,0:T(8,128)(2,1)S(1)} collective-permute-done((bf16[128,2048]{1,0:T(8,128)(2,1)S(1)}, bf16[128,2048]{1,0:T(8,128)(2,1)S(1)}, u32[]{:S(2)}, u32[]{:S(2)}) %collective-permute-start.50) | collective-permute-done | bytes 524320 | tf_op jit(solution)/shard_map/ppermute | solution.py:1083
  423.7 5.2 %collective-permute-done.54 = bf16[2,64,1024]{2,1,0:T(8,128)(2,1)S(1)} collective-permute-done((bf16[2,64,1024]{2,1,0:T(8,128)(2,1)S(1)}, bf16[2,64,1024]{2,1,0:T(8,128)(2,1)S(1)}, u32[]{:S(2)}, u32[]{:S(2)}) %collective-permute-start.54) | collective-permute-done | bytes 262176 | tf_op jit(solution)/shard_map/ppermute | solution.py:1083
  428.9 16.0 %collective-permute-done.56 = bf16[2,208,512]{2,1,0:T(8,128)(2,1)S(1)} collective-permute-done((bf16[2,208,512]{2,1,0:T(8,128)(2,1)S(1)}, bf16[2,208,512]{2,1,0:T(8,128)(2,1)S(1)}, u32[]{:S(2)}, u32[]{:S(2)}) %collective-permute-start.56) | collective-permute-done | bytes 426016 | tf_op jit(solution)/shard_map/ppermute | solution.py:1083
  451.0 8.7 %collective-permute-done.60 = bf16[208,512]{1,0:T(8,128)(2,1)} collective-permute-done((bf16[208,512]{1,0:T(8,128)(2,1)}, bf16[208,512]{1,0:T(8,128)(2,1)}, u32[]{:S(2)}, u32[]{:S(2)}) %collective-permute-start.60) | collective-permute-done | bytes 213024 | tf_op jit(solution)/shard_map/ppermute | solution.py:1083
  (351 shorter events, 172.1 us)
Async XLA Ops:
  5.9 29.9 %collective-permute-start.8 = (bf16[1,3,64,1024]{3,2,1,0:T(8,128)(2,1)S(1)}, bf16[1,3,64,1024]{3,2,1,0:T(8,128)(2,1)S(1)}, u32[]{:S(2)}, u32[]{:S(2)}) collective-permute-start(bf16[1,3,64,1024]{3,2,1,0:T(8,128)(2,1)S(1)} %get-tuple-element.301), channel_id=1, source_target_pairs={{16,28},{17,29},{18,30},{19,31},{20,24},{21,25},{22,26},{23,27},{2... | collective-permute-start | bytes 1179656 | tf_op jit(solution)/shard_map/ppermute | solution.py:1083
  61.5 42.7 %collective-permute-start.20 = (bf16[3,1024,512]{2,1,0:T(8,128)(2,1)}, bf16[3,1024,512]{2,1,0:T(8,128)(2,1)}, u32[]{:S(2)}, u32[]{:S(2)}) collective-permute-start(bf16[3,1024,512]{2,1,0:T(8,128)(2,1)} %bitcast.201), channel_id=1, source_target_pairs={{0,1},{1,0},{2,3},{3,2},{4,5},{5,4},{6,7},{7,6},{8,9},{9,8},{10,11... | collective-permute-start | bytes 9437192 | tf_op jit(solution)/shard_map/ppermute | solution.py:1083
  68.7 28.4 %collective-permute-start.13 = (s32[3,256]{1,0:T(4,128)S(1)}, s32[3,256]{1,0:T(4,128)S(1)}, u32[]{:S(2)}, u32[]{:S(2)}) collective-permute-start(s32[3,256]{1,0:T(4,128)S(1)} %reshape.396), channel_id=1, source_target_pairs={{0,1},{1,0},{2,3},{3,2},{4,5},{5,4},{6,7},{7,6},{8,9},{9,8},{10,11... | collective-permute-start | bytes 9224 | tf_op jit(solution)/shard_map/ppermute | solution.py:1083
  68.8 31.4 %collective-permute-start.14 = (bf16[768,1024]{1,0:T(8,128)(2,1)}, bf16[768,1024]{1,0:T(8,128)(2,1)S(1)}, u32[]{:S(2)}, u32[]{:S(2)}) collective-permute-start(bf16[768,1024]{1,0:T(8,128)(2,1)} %bitcast.20.cot_ref.left), channel_id=1, source_target_pairs={{0,1},{1,0},{2,3},{3,2},{4,5},{5,4},{6,7},{7,6},{8,9},{9,8},{10,11... | collective-permute-start | bytes 4718600 | tf_op jit(solution)/shard_map/ppermute | solution.py:1083
  76.9 28.0 %collective-permute-start.19 = (bf16[256,1024]{1,0:T(8,128)(2,1)}, bf16[256,1024]{1,0:T(8,128)(2,1)}, u32[]{:S(2)}, u32[]{:S(2)}) collective-permute-start(bf16[256,1024]{1,0:T(8,128)(2,1)} %get-tuple-element.148), channel_id=1, source_target_pairs={{0,16},{1,17},{2,18},{3,19},{4,20},{5,21},{6,22},{7,23},{8,24},{9,... | collective-permute-start | bytes 1572872 | tf_op jit(solution)/shard_map/ppermute | solution.py:1095
  102.9 56.7 %collective-permute-start.24 = (bf16[4,64,1024]{2,1,0:T(8,128)(2,1)}, bf16[4,64,1024]{2,1,0:T(8,128)(2,1)}, u32[]{:S(2)}, u32[]{:S(2)}) collective-permute-start(bf16[4,64,1024]{2,1,0:T(8,128)(2,1)} %constant_dynamic-update-slice_fusion.8), channel_id=1, source_target_pairs={{0,16},{1,17},{2,18},{3,19},{4,20},{5,21},{6,22},{7,23},{8,24},{9,... | collective-permute-start | bytes 1572872 | tf_op jit(solution)/shard_map/ppermute | solution.py:1095
  191.0 65.3 %collective-permute-start.30 = (bf16[256,1024]{1,0:T(8,128)(2,1)}, bf16[256,1024]{1,0:T(8,128)(2,1)}, u32[]{:S(2)}, u32[]{:S(2)}) collective-permute-start(bf16[256,1024]{1,0:T(8,128)(2,1)} %get-tuple-element.175.left), channel_id=1, source_target_pairs={{0,1},{1,0},{2,3},{3,2},{4,5},{5,4},{6,7},{7,6},{8,9},{9,8},{10,11... | collective-permute-start | bytes 1572872 | tf_op jit(solution)/shard_map/ppermute | solution.py:1083
  191.1 30.1 %collective-permute-start.31 = (bf16[256,2048]{1,0:T(8,128)(2,1)S(1)}, bf16[256,2048]{1,0:T(8,128)(2,1)}, u32[]{:S(2)}, u32[]{:S(2)}) collective-permute-start(bf16[256,2048]{1,0:T(8,128)(2,1)S(1)} %copy-done.42), channel_id=1, source_target_pairs={{0,1},{1,0},{2,3},{3,2},{4,5},{5,4},{6,7},{7,6},{8,9},{9,8},{10,11... | collective-permute-start | bytes 3145736 | tf_op jit(solution)/shard_map/ppermute | solution.py:1083
  211.9 36.4 %collective-permute-start.35 = (bf16[256,2048]{1,0:T(8,128)(2,1)}, bf16[256,2048]{1,0:T(8,128)(2,1)}, u32[]{:S(2)}, u32[]{:S(2)}) collective-permute-start(bf16[256,2048]{1,0:T(8,128)(2,1)} %get-tuple-element.185), channel_id=1, source_target_pairs={{0,1},{1,0},{2,3},{3,2},{4,5},{5,4},{6,7},{7,6},{8,9},{9,8},{10,11... | collective-permute-start | bytes 3145736 | tf_op jit(solution)/shard_map/ppermute | solution.py:1083
  216.5 30.2 %collective-permute-start.33 = (bf16[1,3,64,1024]{3,2,1,0:T(8,128)(2,1)S(1)}, bf16[1,3,64,1024]{3,2,1,0:T(8,128)(2,1)S(1)}, u32[]{:S(2)}, u32[]{:S(2)}) collective-permute-start(bf16[1,3,64,1024]{3,2,1,0:T(8,128)(2,1)S(1)} %get-tuple-element.304), channel_id=1, source_target_pairs={{16,24},{17,25},{18,26},{19,27},{20,28},{21,29},{22,30},{23,31},{2... | collective-permute-start | bytes 1179656 | tf_op jit(solution)/shard_map/ppermute | solution.py:1083
  248.3 55.2 %collective-permute-start.39 = (bf16[2,2,128,2048]{3,2,1,0:T(8,128)(2,1)}, bf16[2,2,128,2048]{3,2,1,0:T(8,128)(2,1)S(1)}, u32[]{:S(2)}, u32[]{:S(2)}) collective-permute-start(bf16[2,2,128,2048]{3,2,1,0:T(8,128)(2,1)} %get-tuple-element.204), channel_id=1, source_target_pairs={{0,4},{1,5},{2,6},{3,7},{4,0},{5,1},{6,2},{7,3},{8,12},{9,13},{10,... | collective-permute-start | bytes 6291464 | tf_op jit(solution)/shard_map/ppermute | solution.py:1083
  261.6 45.8 %collective-permute-start.40 = (bf16[4,128,2048]{2,1,0:T(8,128)(2,1)}, bf16[4,128,2048]{2,1,0:T(8,128)(2,1)}, u32[]{:S(2)}, u32[]{:S(2)}) collective-permute-start(bf16[4,128,2048]{2,1,0:T(8,128)(2,1)} %get-tuple-element.205), channel_id=1, source_target_pairs={{0,2},{1,3},{2,0},{3,1},{4,6},{5,7},{6,4},{7,5},{8,10},{9,11},{10,... | collective-permute-start | bytes 6291464 | tf_op jit(solution)/shard_map/ppermute | solution.py:1083
  283.1 41.8 %collective-permute-start.46 = (bf16[2,4,3,64,512]{4,3,2,1,0:T(8,128)(2,1)}, bf16[2,4,3,64,512]{4,3,2,1,0:T(8,128)(2,1)}, u32[]{:S(2)}, u32[]{:S(2)}) collective-permute-start(bf16[2,4,3,64,512]{4,3,2,1,0:T(8,128)(2,1)} %get-tuple-element.220), channel_id=1, source_target_pairs={{16,0},{17,1},{18,2},{19,3},{20,4},{21,5},{22,6},{23,7},{24,8},{25... | collective-permute-start | bytes 4718600 | tf_op jit(solution)/shard_map/ppermute | solution.py:1098
  307.5 58.8 %collective-permute-start.42 = (bf16[4,4,2,128,256]{4,3,2,1,0:T(8,128)(2,1)S(1)}, bf16[4,4,2,128,256]{4,3,2,1,0:T(8,128)(2,1)S(1)}, u32[]{:S(2)}, u32[]{:S(2)}) collective-permute-start(bf16[4,4,2,128,256]{4,3,2,1,0:T(8,128)(2,1)S(1)} %maximum_select_fusion.1), channel_id=1, source_target_pairs={{0,2},{1,3},{2,0},{3,1},{4,6},{5,7},{6,4},{7,5},{8,10},{9,11},{10,... | collective-permute-start | bytes 6291464 | tf_op jit(solution)/shard_map/ppermute | solution.py:1083
  311.5 36.4 %collective-permute-start.43 = (bf16[2,128,2048]{2,1,0:T(8,128)(2,1)S(1)}, bf16[2,128,2048]{2,1,0:T(8,128)(2,1)S(1)}, u32[]{:S(2)}, u32[]{:S(2)}) collective-permute-start(bf16[2,128,2048]{2,1,0:T(8,128)(2,1)S(1)} %slice.235), channel_id=1, source_target_pairs={{0,4},{1,5},{2,6},{3,7},{4,0},{5,1},{6,2},{7,3},{8,12},{9,13},{10,... | collective-permute-start | bytes 3145736 | tf_op jit(solution)/shard_map/ppermute | solution.py:1083
  319.6 46.7 %collective-permute-start.44 = (bf16[2,128,2048]{2,1,0:T(8,128)(2,1)S(1)}, bf16[2,128,2048]{2,1,0:T(8,128)(2,1)S(1)}, u32[]{:S(2)}, u32[]{:S(2)}) collective-permute-start(bf16[2,128,2048]{2,1,0:T(8,128)(2,1)S(1)} %slice_bitcast_fusion.1), channel_id=1, source_target_pairs={{0,8},{1,9},{2,10},{3,11},{4,12},{5,13},{6,14},{7,15},{8,0},{9,1},... | collective-permute-start | bytes 3145736 | tf_op jit(solution)/shard_map/ppermute | solution.py:1083
  323.0 43.3 %collective-permute-start.45 = (bf16[256,1024]{1,0:T(8,128)(2,1)S(1)}, bf16[256,1024]{1,0:T(8,128)(2,1)S(1)}, u32[]{:S(2)}, u32[]{:S(2)}) collective-permute-start(bf16[256,1024]{1,0:T(8,128)(2,1)S(1)} %slice.314), channel_id=1, source_target_pairs={{0,2},{1,3},{2,0},{3,1},{4,6},{5,7},{6,4},{7,5},{8,10},{9,11},{10,... | collective-permute-start | bytes 1572872 | tf_op jit(solution)/shard_map/ppermute | solution.py:1083
  324.9 55.7 %collective-permute-start.58 = (bf16[4,64,1024]{2,1,0:T(8,128)(2,1)S(1)}, bf16[4,64,1024]{2,1,0:T(8,128)(2,1)}, u32[]{:S(2)}, u32[]{:S(2)}) collective-permute-start(bf16[4,64,1024]{2,1,0:T(8,128)(2,1)S(1)} %broadcast_select_fusion.6), channel_id=1, source_target_pairs={{0,1},{1,0},{2,3},{3,2},{4,5},{5,4},{6,7},{7,6},{8,9},{9,8},{10,11... | collective-permute-start | bytes 1572872 | tf_op jit(solution)/shard_map/ppermute | solution.py:1083
  347.9 34.5 %collective-permute-start.52 = (bf16[4,3,64,1024]{3,2,1,0:T(8,128)(2,1)}, bf16[4,3,64,1024]{3,2,1,0:T(8,128)(2,1)}, u32[]{:S(2)}, u32[]{:S(2)}) collective-permute-start(bf16[4,3,64,1024]{3,2,1,0:T(8,128)(2,1)} %constant_dynamic-update-slice_fusion.5), channel_id=1, source_target_pairs={{16,0},{17,1},{18,2},{19,3},{20,4},{21,5},{22,6},{23,7},{24,8},{25... | collective-permute-start | bytes 4718600 | tf_op jit(solution)/shard_map/ppermute | solution.py:1098
  368.2 43.7 %collective-permute-start.48 = (bf16[2,4,2,128,256]{4,3,2,1,0:T(8,128)(2,1)}, bf16[2,4,2,128,256]{4,3,2,1,0:T(8,128)(2,1)}, u32[]{:S(2)}, u32[]{:S(2)}) collective-permute-start(bf16[2,4,2,128,256]{4,3,2,1,0:T(8,128)(2,1)} %slice.202), channel_id=1, source_target_pairs={{0,4},{1,5},{2,6},{3,7},{4,0},{5,1},{6,2},{7,3},{8,12},{9,13},{10,... | collective-permute-start | bytes 3145736 | tf_op jit(solution)/shard_map/ppermute | solution.py:1083
  369.6 36.0 %collective-permute-start.49 = (bf16[128,2048]{1,0:T(8,128)(2,1)}, bf16[128,2048]{1,0:T(8,128)(2,1)}, u32[]{:S(2)}, u32[]{:S(2)}) collective-permute-start(bf16[128,2048]{1,0:T(8,128)(2,1)} %slice_bitcast_fusion.8), channel_id=1, source_target_pairs={{0,8},{1,9},{2,10},{3,11},{4,12},{5,13},{6,14},{7,15},{8,0},{9,1},... | collective-permute-start | bytes 1572872 | tf_op jit(solution)/shard_map/ppermute | solution.py:1083
  380.3 31.6 %collective-permute-start.51 = (bf16[4,208,512]{2,1,0:T(8,128)(2,1)S(1)}, bf16[4,208,512]{2,1,0:T(8,128)(2,1)S(1)}, u32[]{:S(2)}, u32[]{:S(2)}) collective-permute-start(bf16[4,208,512]{2,1,0:T(8,128)(2,1)S(1)} %slice_bitcast_fusion.2), channel_id=1, source_target_pairs={{0,2},{1,3},{2,0},{3,1},{4,6},{5,7},{6,4},{7,5},{8,10},{9,11},{10,... | collective-permute-start | bytes 2555912 | tf_op jit(solution)/shard_map/ppermute | solution.py:1083
  380.6 31.3 %collective-permute-start.50 = (bf16[128,2048]{1,0:T(8,128)(2,1)S(1)}, bf16[128,2048]{1,0:T(8,128)(2,1)S(1)}, u32[]{:S(2)}, u32[]{:S(2)}) collective-permute-start(bf16[128,2048]{1,0:T(8,128)(2,1)S(1)} %copy-done.32), channel_id=1, source_target_pairs={{0,2},{1,3},{2,0},{3,1},{4,6},{5,7},{6,4},{7,5},{8,10},{9,11},{10,... | collective-permute-start | bytes 1572872 | tf_op jit(solution)/shard_map/ppermute | solution.py:1083
  416.7 28.2 %collective-permute-start.55 = (bf16[4,2,128,256]{3,2,1,0:T(8,128)(2,1)S(1)}, bf16[4,2,128,256]{3,2,1,0:T(8,128)(2,1)S(1)}, u32[]{:S(2)}, u32[]{:S(2)}) collective-permute-start(bf16[4,2,128,256]{3,2,1,0:T(8,128)(2,1)S(1)} %slice_bitcast_fusion.17), channel_id=1, source_target_pairs={{0,8},{1,9},{2,10},{3,11},{4,12},{5,13},{6,14},{7,15},{8,0},{9,1},... | collective-permute-start | bytes 1572872 | tf_op jit(solution)/shard_map/ppermute | solution.py:1083
  (88 other events, 810.3 us)
